TPU v7x, 256 devices: a whole 4x4x8 slice. The times are simulated.
256 devices in a mesh: seq: 128 (over x_lo, y, z, core), rep: 2 (over x_hi).
Axes of the slice: x: 4 (x_hi: 2, x_lo: 2; x = x_hi * 2 + x_lo), y: 4, z: 8, core: 2. Of those that a mesh axis runs over, the one named last changes fastest.
Arguments:
- tokens: bfloat16 [2, 32768, 2304], P('rep', 'seq'), may hold values from -24 to 24
- window_ids: int32 [2, 32768], P('rep', 'seq'), may hold values from 0 to 1023, as said below
- cotangent: bfloat16 [2, 32768, 2304], P('rep', 'seq'), may hold values from -24 to 24
- modulation: float32 [6, 2304], replicated, may hold values from -4 to 4
- w_qkv: bfloat16 [2, 2304, 768], replicated
- w_out: bfloat16 [2, 256, 2304], replicated, may hold values from -0.375 to 0.375
Outputs:
- grad_tokens: bfloat16 [2, 32768, 2304], P('rep', 'seq')
- grad_qkv: bfloat16 [2, 2304, 768], P(None, ('seq', 'rep'))
- grad_out: bfloat16 [2, 256, 2304], P(None, None, ('seq', 'rep'))
Inputs may be any that keep to these rules, and one draw needn't show every extreme that they name: `window_ids`: each id names exactly 64 tokens, all inside one aligned block of 256 tokens of a group; the ids of the b-th such block (groups in order) are b * 4 to (b + 1) * 4 - 1.
All inputs are finite; a program needn't handle non-finite values.
Results may differ from a plain program's by a relative error of at most 0.027.
Values may be sent and summed in bfloat16 or wider, within the bound.
A program may use at most 128 MiB of HBM per device.

v0:
```python
import math

import jax
import jax.numpy as jnp
from jax import lax
from jax.sharding import PartitionSpec as P

HD = 128
HEADS = 2
FRAMES = 8


epsilon = 1e-06


def normalize(values):
    values = values.astype(jnp.float32)
    centered = values - jnp.mean(values, axis=-1, keepdims=True)
    inv_std = lax.rsqrt(jnp.mean(centered * centered, axis=-1, keepdims=True) + epsilon)
    return (centered * inv_std, inv_std)


def norm_back(d_normed, normed, inv_std):
    return inv_std * (
        d_normed
        - jnp.mean(d_normed, axis=-1, keepdims=True)
        - normed * jnp.mean(d_normed * normed, axis=-1, keepdims=True)
    )


def contract_rows(left, right):
    return lax.dot_general(
        left, right, (((0,), (0,)), ((), ())), preferred_element_type=jnp.float32
    )


def times_transposed(left, right):
    return lax.dot_general(
        left, right, (((1,), (1,)), ((), ())), preferred_element_type=jnp.float32
    )


def split_heads(packed):
    groups, length, width = packed.shape
    parts = packed.reshape(groups, length, 3, HEADS, HD)
    return (parts[:, :, 0], parts[:, :, 1], parts[:, :, 2])


def attend(packed, mask):
    query, key_part, value_part = split_heads(packed)
    scores = jnp.einsum(
        "gihd,gjhd->ghij", query, key_part, preferred_element_type=jnp.float32
    ) * HD ** (-0.5)
    if mask is not None:
        scores = jnp.where(mask[:, None], scores, -1e30)
    top_score = jnp.max(scores, axis=-1, keepdims=True)
    expd = jnp.exp(scores - top_score)
    attn_probs = expd / jnp.sum(expd, axis=-1, keepdims=True)
    rounded = attn_probs.astype(jnp.bfloat16)
    result = jnp.einsum("ghij,gjhd->gihd", rounded, value_part, preferred_element_type=jnp.float32)
    groups, length = (packed.shape[0], packed.shape[1])
    return (result.astype(jnp.bfloat16).reshape(groups, length, HEADS * HD), attn_probs)


def attend_back(packed, attn_probs, d_att):
    query, key_part, value_part = split_heads(packed)
    groups, length = (packed.shape[0], packed.shape[1])
    d_heads = d_att.reshape(groups, length, HEADS, HD)
    rounded = attn_probs.astype(jnp.bfloat16)
    d_value = jnp.einsum("ghij,gihd->gjhd", rounded, d_heads, preferred_element_type=jnp.float32)
    d_prob = jnp.einsum("gihd,gjhd->ghij", d_heads, value_part, preferred_element_type=jnp.float32)
    d_score = attn_probs * (d_prob - jnp.sum(attn_probs * d_prob, axis=-1, keepdims=True))
    d_score = d_score.astype(jnp.bfloat16)
    d_query = jnp.einsum(
        "ghij,gjhd->gihd", d_score, key_part, preferred_element_type=jnp.float32
    ) * HD ** (-0.5)
    d_key = jnp.einsum(
        "ghij,gihd->gjhd", d_score, query, preferred_element_type=jnp.float32
    ) * HD ** (-0.5)
    stacked = jnp.stack([d_query, d_key, d_value], axis=2)
    return stacked.astype(jnp.bfloat16).reshape(groups, length, 3 * HEADS * HD)


def to_groups(values):
    total, width = values.shape
    return values.reshape(FRAMES, total // FRAMES, width).transpose(1, 0, 2)


def from_groups(values):
    pixel_count, frame_count, width = values.shape
    return values.transpose(1, 0, 2).reshape(frame_count * pixel_count, width)


def project_in(block_in, mod_rows, weight_in):
    normed, inv_std = normalize(block_in)
    hidden = (normed * (1.0 + mod_rows[1]) + mod_rows[0]).astype(jnp.bfloat16)
    packed = jnp.dot(hidden, weight_in, preferred_element_type=jnp.float32).astype(jnp.bfloat16)
    return (normed, inv_std, hidden, packed)


def output_side(d_block, mod_rows, weight_out, attended):
    gated = (mod_rows[2] * d_block.astype(jnp.float32)).astype(jnp.bfloat16)
    d_att = times_transposed(gated, weight_out).astype(jnp.bfloat16)
    sum_out = contract_rows(attended, gated)
    return (d_att, sum_out)


def input_side(d_block, d_packed, mod_rows, weight_in, hidden, normed, inv_std):
    sum_qkv = contract_rows(hidden, d_packed)
    d_hidden = times_transposed(d_packed, weight_in)
    d_in = (
        d_block.astype(jnp.float32) + norm_back(d_hidden * (1.0 + mod_rows[1]), normed, inv_std)
    ).astype(jnp.bfloat16)
    return (d_in, sum_qkv)


def local(tokens, window_ids, cotangent, modulation, w_qkv, w_out):
    block_rows = tokens[0]
    local_ids = window_ids[0]
    d_top = cotangent[0]
    mod_s = modulation[0:3]
    mod_t = modulation[3:6]
    mask = (local_ids[:, None] == local_ids[None, :])[None]
    normed_s, inv_s, hidden_s, packed_s = project_in(block_rows, mod_s, w_qkv[0])
    att_groups, probs_s = attend(packed_s[None], mask)
    attended_s = att_groups[0]
    middle = (
        block_rows.astype(jnp.float32)
        + mod_s[2] * jnp.dot(attended_s, w_out[0], preferred_element_type=jnp.float32)
    ).astype(jnp.bfloat16)
    middle_pix = lax.all_to_all(middle, "seq", split_axis=0, concat_axis=0, tiled=True)
    normed_t, inv_t, hidden_t, packed_t = project_in(middle_pix, mod_t, w_qkv[1])
    temporal_groups, probs_t = attend(to_groups(packed_t), None)
    attended_t = from_groups(temporal_groups)
    d_pix = lax.all_to_all(d_top, "seq", split_axis=0, concat_axis=0, tiled=True)
    d_att_t, sum_out_t = output_side(d_pix, mod_t, w_out[1], attended_t)
    d_packed_t = from_groups(attend_back(to_groups(packed_t), probs_t, to_groups(d_att_t)))
    d_mid_pix, sum_qkv_t = input_side(d_pix, d_packed_t, mod_t, w_qkv[1], hidden_t, normed_t, inv_t)
    d_middle = lax.all_to_all(d_mid_pix, "seq", split_axis=0, concat_axis=0, tiled=True)
    d_att_s, sum_out_s = output_side(d_middle, mod_s, w_out[0], attended_s)
    d_packed_s = attend_back(packed_s[None], probs_s, d_att_s[None])[0]
    d_tokens, sum_qkv_s = input_side(
        d_middle, d_packed_s, mod_s, w_qkv[0], hidden_s, normed_s, inv_s
    )
    summed_qkv, summed_out = (
        lax.psum_scatter(
            jnp.stack([sum_qkv_s, sum_qkv_t]), ("seq", "rep"), scatter_dimension=1, tiled=True
        ),
        lax.psum_scatter(
            jnp.stack([sum_out_s, sum_out_t]), ("seq", "rep"), scatter_dimension=2, tiled=True
        ),
    )
    token_total = block_rows.shape[0] * lax.axis_size("seq") * lax.axis_size("rep")
    factor = 1.0 / math.sqrt(token_total)
    return (
        d_tokens[None],
        (summed_qkv * factor).astype(jnp.bfloat16),
        (summed_out * factor).astype(jnp.bfloat16),
    )


def solution(mesh):
    in_specs = (P("rep", "seq", None), P("rep", "seq"), P("rep", "seq", None), P(), P(), P())
    out_specs = (
        P("rep", "seq", None),
        P(None, ("seq", "rep"), None),
        P(None, None, ("seq", "rep")),
    )
    return jax.shard_map(local, mesh=mesh, in_specs=in_specs, out_specs=out_specs, check_vma=False)
```

profile of v0, /device:TPU:1, one launch (start us, length us, event | category | flops | bytes accessed | tf_op | source)
XLA Modules:
  0.0 570.0 jit_solution(15714392514945207808)
XLA Ops:
  12.5 3.2 fusion.30
  21.8 14.9 %all-to-all-start.1 = ((bf16[128,2,2304]{2,1,0:T(2,128)(2,1)}), bf16[128,2,2304]{2,1,0:T(2,128)(2,1)S(1)}, u32[]{:S(2)}, u32[]{:S(2)}) async-start(bf16[128,2,2304]{2,1,0:T(2,128)(2,1)} %all_to_all.20), calls=%async_computation.1 | async-start | bytes 2359296 | tf_op jit(solution)/shard_map/all_to_all | solution.py:131
  38.0 30.1 %all-to-all-done.1 = bf16[128,2,2304]{2,1,0:T(2,128)(2,1)S(1)} async-done(((bf16[128,2,2304]{2,1,0:T(2,128)(2,1)}), bf16[128,2,2304]{2,1,0:T(2,128)(2,1)S(1)}, u32[]{:S(2)}, u32[]{:S(2)}) %all-to-all-start.1) | async-done | bytes 1179680 | tf_op jit(solution)/shard_map/all_to_all | solution.py:131
  68.0 8.0 %all-to-all-start = ((bf16[128,2,2304]{2,1,0:T(2,128)(2,1)}), bf16[128,2,2304]{2,1,0:T(2,128)(2,1)S(1)}, u32[]{:S(2)}, u32[]{:S(2)}) async-start(bf16[128,2,2304]{2,1,0:T(2,128)(2,1)} %all_to_all.18), calls=%async_computation | async-start | bytes 2359296 | tf_op jit(solution)/shard_map/all_to_all | solution.py:135
  83.9 23.5 %all-to-all-done = bf16[128,2,2304]{2,1,0:T(2,128)(2,1)S(1)} async-done(((bf16[128,2,2304]{2,1,0:T(2,128)(2,1)}), bf16[128,2,2304]{2,1,0:T(2,128)(2,1)S(1)}, u32[]{:S(2)}, u32[]{:S(2)}) %all-to-all-start) | async-done | bytes 1179680 | tf_op jit(solution)/shard_map/all_to_all | solution.py:135
  107.4 2.6 multiply_convert_fusion.1
  110.0 3.6 convert_element_type.175
  113.7 2.8 fusion.55
  116.5 3.0 add_convert_fusion.1
  119.4 3.7 convert_element_type.171
  123.1 3.4 fusion.33
  135.8 5.3 fusion.89
  143.3 3.9 add_convert_fusion
  148.5 8.0 %all-to-all-start.2 = ((bf16[128,2,2304]{2,1,0:T(2,128)(2,1)}), bf16[128,2,2304]{2,1,0:T(2,128)(2,1)S(1)}, u32[]{:S(2)}, u32[]{:S(2)}) async-start(bf16[128,2,2304]{2,1,0:T(2,128)(2,1)} %all_to_all.22), calls=%async_computation.2 | async-start | bytes 2359296 | tf_op jit(solution)/shard_map/all_to_all | solution.py:139
  158.0 3.3 convolution_bitcast_fusion.2
  161.4 4.1 convolution_bitcast_fusion
  165.4 22.5 %all-to-all-done.2 = bf16[128,2,2304]{2,1,0:T(2,128)(2,1)S(1)} async-done(((bf16[128,2,2304]{2,1,0:T(2,128)(2,1)}), bf16[128,2,2304]{2,1,0:T(2,128)(2,1)S(1)}, u32[]{:S(2)}, u32[]{:S(2)}) %all-to-all-start.2) | async-done | bytes 1179680 | tf_op jit(solution)/shard_map/all_to_all | solution.py:139
  190.5 2.9 convert_element_type.187
  202.9 4.3 convolution_bitcast_fusion.1
  207.3 11.1 %pad_maximum_fusion = f32[2,2304,768]{2,1,0:T(8,128)} fusion(f32[1,2304,768]{2,1,0:T(8,128)} %convolution_bitcast_fusion, f32[1,2304,768]{2,1,0:T(8,128)} %convolution_bitcast_fusion.1), kind=kLoop, calls=%fused_computation.2 | loop fusion | flops 3538944 | bytes 28311552 | tf_op jit(solution)/shard_map/stack | solution.py:147
  218.3 32.1 %copy.88 = f32[2,2304,768]{2,0,1:T(2,128)} copy(f32[2,2304,768]{2,1,0:T(8,128)} %pad_maximum_fusion) | data formatting | bytes 28311552 | tf_op jit(solution)/shard_map/stack | solution.py:147
  252.9 8.1 %copy.91 = f32[2,256,2304]{1,0,2:T(2,128)} copy(f32[2,256,2304]{2,1,0:T(8,128)} %pad_maximum_fusion.1) | data formatting | bytes 9437184 | tf_op jit(solution)/shard_map/stack | solution.py:150
  262.6 3.7 fusion.88
  268.1 292.2 %all-reduce.5.cloned.1.call-done = (f32[2,2304,768]{2,0,1:T(2,128)}, f32[2,256,2304]{1,0,2:T(2,128)}) async-done(((f32[2,2304,768]{2,0,1:T(2,128)}, f32[2,256,2304]{1,0,2:T(2,128)}), (f32[2,2304,768]{2,0,1:T(2,128)}, f32[2,256,2304]{1,0,2:T(2,128)})) %all-reduce.5.cloned.1.call-update) | async-done | bytes 18874384
  (118 shorter events, 55.2 us)
Async XLA Ops:
  7.2 5.4 copy-start
  9.2 6.5 %copy-start.20 = (f32[2304]{0:T(1024)}, f32[2304]{0:T(1024)S(1)}, u32[]{:S(2)}) copy-start(f32[2304]{0:T(1024)S(1)} %get-tuple-element.17) | copy-start | bytes 27652
  9.2 8.9 %copy-start.23 = (f32[2304]{0:T(1024)}, f32[2304]{0:T(1024)S(1)}, u32[]{:S(2)}) copy-start(f32[2304]{0:T(1024)S(1)} %get-tuple-element.19) | copy-start | bytes 27652
  12.5 3.3 copy-start.27
  12.5 3.8 copy-start.30
  20.5 16.2 %copy-start.6 = (bf16[1,256,2304]{2,1,0:T(8,128)(2,1)S(1)}, bf16[1,256,2304]{2,1,0:T(8,128)(2,1)}, u32[]{:S(2)}) copy-start(bf16[1,256,2304]{2,1,0:T(8,128)(2,1)} %param.8) | copy-start | bytes 3538948
  21.8 46.2 %all-to-all-start.1 = ((bf16[128,2,2304]{2,1,0:T(2,128)(2,1)}), bf16[128,2,2304]{2,1,0:T(2,128)(2,1)S(1)}, u32[]{:S(2)}, u32[]{:S(2)}) async-start(bf16[128,2,2304]{2,1,0:T(2,128)(2,1)} %all_to_all.20), calls=%async_computation.1 | async-start | bytes 2359296 | tf_op jit(solution)/shard_map/all_to_all | solution.py:131
  68.0 39.4 %all-to-all-start = ((bf16[128,2,2304]{2,1,0:T(2,128)(2,1)}), bf16[128,2,2304]{2,1,0:T(2,128)(2,1)S(1)}, u32[]{:S(2)}, u32[]{:S(2)}) async-start(bf16[128,2,2304]{2,1,0:T(2,128)(2,1)} %all_to_all.18), calls=%async_computation | async-start | bytes 2359296 | tf_op jit(solution)/shard_map/all_to_all | solution.py:135
  113.6 2.8 copy-start.8
  113.7 2.8 copy-start.9
  113.7 2.8 copy-start.24
  113.7 2.8 copy-start.25
  130.2 2.6 copy-start.15
  130.2 2.6 copy-start.26
  130.2 2.7 copy-start.7
  148.5 39.4 %all-to-all-start.2 = ((bf16[128,2,2304]{2,1,0:T(2,128)(2,1)}), bf16[128,2,2304]{2,1,0:T(2,128)(2,1)S(1)}, u32[]{:S(2)}, u32[]{:S(2)}) async-start(bf16[128,2,2304]{2,1,0:T(2,128)(2,1)} %all_to_all.22), calls=%async_computation.2 | async-start | bytes 2359296 | tf_op jit(solution)/shard_map/all_to_all | solution.py:139
  156.5 4.8 copy-start.4
  156.5 403.8 %all-reduce.5.cloned.1.call-start = ((), (), s32[]{:S(2)}) async-start(), calls=%async_computation.3 | async-start | bytes 37748736
  156.6 4.8 copy-start.5
  198.1 2.6 copy-start.12
  198.1 2.8 copy-start.17
  218.3 32.1 %copy-start.2 = (f32[1,256,2304]{2,1,0:T(8,128)S(1)}, f32[1,256,2304]{2,1,0:T(8,128)}, u32[]{:S(2)}) copy-start(f32[1,256,2304]{2,1,0:T(8,128)} %convolution_bitcast_fusion.2) | copy-start | bytes 7077892
  218.3 32.1 %copy-start.3 = (f32[1,256,2304]{2,1,0:T(8,128)S(1)}, f32[1,256,2304]{2,1,0:T(8,128)}, u32[]{:S(2)}) copy-start(f32[1,256,2304]{2,1,0:T(8,128)} %convolution_bitcast_fusion.3) | copy-start | bytes 7077892
  262.6 3.7 copy-start.1
  (12 other events, 20.3 us)
Sparse Core Ops, SparseCore 0:
  261.1 299.2 all-reduce.4
where the time goes:
time: 572 us; the launch traced here: 570 us
  waiting for transfers between devices  368 us (64%)
  local copies, waits for them, and re-layouts  65.1 us (11%)
  matrix products  49.3 us (9%)
  other arithmetic  41.9 us (7%)
  starting transfers between devices  30.9 us (5%)
  between operations  14.6 us (3%)
    unnamed x2, waiting for transfers between devices  292 us
    another operation x1, local copies, waits for them, and re-layouts, local(): jnp.stack([sum_qkv_s, sum_qkv_t])  32.1 us
    all_to_all x1, waiting for transfers between devices, local(): lax.all_to_all(middle, 'seq', split_axis=0, concat_axis=0, tiled=True)  30.1 us
    all_to_all x1, waiting for transfers between devices, local(): lax.all_to_all(d_top, 'seq', split_axis=0, concat_axis=0, tiled=True)  23.5 us
    all_to_all x1, waiting for transfers between devices, local(): lax.all_to_all(d_mid_pix, 'seq', split_axis=0, concat_axis=0, tiled=True)  22.5 us
    all_to_all x1, starting transfers between devices, local(): lax.all_to_all(middle, 'seq', split_axis=0, concat_axis=0, tiled=True)  14.9 us
    dot_general x4, matrix products, times_transposed(): lax.dot_general(left, right, (((1,), (1,)), ((), ())), preferred_element_...  14.3 us
    dot_general x4, matrix products, contract_rows(): lax.dot_general(left, right, (((0,), (0,)), ((), ())), preferred_element_...  13.6 us
  transfers between devices with their start and end apart: 4, of which 4 were waited for; matrix products, arithmetic and copies ran while one was open for 4% of the time, Pallas kernels for 0%

commit v1 on v0

v1 whole, which is shorter than its diff:
```python
import math

import jax
import jax.numpy as jnp
from jax import lax
from jax.sharding import PartitionSpec as P

HD = 128
HEADS = 2
FRAMES = 8
epsilon = 1e-06


def normalize(values):
    values = values.astype(jnp.float32)
    centered = values - jnp.mean(values, axis=-1, keepdims=True)
    inv_std = lax.rsqrt(jnp.mean(centered * centered, axis=-1, keepdims=True) + epsilon)
    return (centered * inv_std, inv_std)


def norm_back(d_normed, normed, inv_std):
    return inv_std * (
        d_normed
        - jnp.mean(d_normed, axis=-1, keepdims=True)
        - normed * jnp.mean(d_normed * normed, axis=-1, keepdims=True)
    )


def contract_rows(left, right):
    return lax.dot_general(
        left, right, (((0,), (0,)), ((), ())), preferred_element_type=jnp.float32
    )


def times_transposed(left, right):
    return lax.dot_general(
        left, right, (((1,), (1,)), ((), ())), preferred_element_type=jnp.float32
    )


def dot(left, right):
    return jnp.dot(left, right, preferred_element_type=jnp.float32)


def head(packed, part, h):
    at = (part * HEADS + h) * HD
    return packed[:, at : at + HD]


def attend(packed, mask):
    probs, outs = [], []
    for h in range(HEADS):
        scores = times_transposed(head(packed, 0, h), head(packed, 1, h)) * HD ** (-0.5)
        scores = jnp.where(mask, scores, -1e30)
        expd = jnp.exp(scores - jnp.max(scores, axis=-1, keepdims=True))
        p = expd / jnp.sum(expd, axis=-1, keepdims=True)
        probs.append(p)
        outs.append(dot(p.astype(jnp.bfloat16), head(packed, 2, h)).astype(jnp.bfloat16))
    return jnp.concatenate(outs, axis=1), probs


def attend_back(packed, probs, d_att):
    dq, dk, dv = [], [], []
    for h in range(HEADS):
        p = probs[h]
        d_out = d_att[:, h * HD : (h + 1) * HD]
        dv.append(contract_rows(p.astype(jnp.bfloat16), d_out))
        dp = times_transposed(d_out, head(packed, 2, h))
        ds = p * (dp - jnp.sum(p * dp, axis=-1, keepdims=True))
        ds = ds.astype(jnp.bfloat16)
        dq.append(dot(ds, head(packed, 1, h)) * HD ** (-0.5))
        dk.append(contract_rows(ds, head(packed, 0, h)) * HD ** (-0.5))
    return jnp.concatenate(dq + dk + dv, axis=1).astype(jnp.bfloat16)


def project_in(block_in, mod_rows, weight_in):
    normed, inv_std = normalize(block_in)
    hidden = (normed * (1.0 + mod_rows[1]) + mod_rows[0]).astype(jnp.bfloat16)
    packed = dot(hidden, weight_in).astype(jnp.bfloat16)
    return (normed, inv_std, hidden, packed)


def gate(d_block, mod_rows):
    return (mod_rows[2] * d_block.astype(jnp.float32)).astype(jnp.bfloat16)


def input_side(d_block, d_packed, mod_rows, weight_in, normed, inv_std):
    d_hidden = times_transposed(d_packed, weight_in)
    return (
        d_block.astype(jnp.float32) + norm_back(d_hidden * (1.0 + mod_rows[1]), normed, inv_std)
    ).astype(jnp.bfloat16)


def local(tokens, window_ids, cotangent, modulation, w_qkv, w_out):
    x = tokens[0]
    ids = window_ids[0]
    d_top = cotangent[0]
    rows = x.shape[0]
    seq = lax.axis_size("seq")
    per_frame = seq // FRAMES
    groups = [[b + per_frame * f for f in range(FRAMES)] for b in range(per_frame)]
    mod_s = modulation[0:3]
    mod_t = modulation[3:6]
    mask_s = ids[:, None] == ids[None, :]
    pixel = lax.rem(jnp.arange(rows, dtype=jnp.int32), rows // FRAMES)
    mask_t = pixel[:, None] == pixel[None, :]

    def exchange(values):
        return lax.all_to_all(
            values, "seq", split_axis=0, concat_axis=0, tiled=True, axis_index_groups=groups
        )

    normed_s, inv_s, hidden_s, packed_s = project_in(x, mod_s, w_qkv[0])
    attended_s, probs_s = attend(packed_s, mask_s)
    middle = (
        x.astype(jnp.float32) + mod_s[2] * dot(attended_s, w_out[0])
    ).astype(jnp.bfloat16)
    normed_t, inv_t, hidden_t, packed_t = project_in(middle, mod_t, w_qkv[1])
    gated_t = gate(d_top, mod_t)
    d_att_t = times_transposed(gated_t, w_out[1]).astype(jnp.bfloat16)
    pix = exchange(jnp.concatenate([packed_t, d_att_t], axis=1))
    wide = 3 * HEADS * HD
    attended_p, probs_p = attend(pix[:, :wide], mask_t)
    d_packed_p = attend_back(pix[:, :wide], probs_p, pix[:, wide:])
    back = exchange(jnp.concatenate([d_packed_p, attended_p], axis=1))
    d_packed_t = back[:, :wide]
    attended_t = back[:, wide:]
    d_middle = input_side(d_top, d_packed_t, mod_t, w_qkv[1], normed_t, inv_t)
    gated_s = gate(d_middle, mod_s)
    d_att_s = times_transposed(gated_s, w_out[0]).astype(jnp.bfloat16)
    d_packed_s = attend_back(packed_s, probs_s, d_att_s)
    d_tokens = input_side(d_middle, d_packed_s, mod_s, w_qkv[0], normed_s, inv_s)

    sums = jnp.concatenate(
        [
            contract_rows(hidden_s, d_packed_s),
            contract_rows(hidden_t, d_packed_t),
            contract_rows(gated_s, attended_s),
            contract_rows(gated_t, attended_t),
        ],
        axis=1,
    ).astype(jnp.bfloat16)
    devices = seq * lax.axis_size("rep")
    features, columns = sums.shape
    own = features // devices
    summed = lax.psum_scatter(
        sums.reshape(devices, own * columns), ("seq", "rep"), scatter_dimension=0, tiled=True
    ).reshape(own, columns).astype(jnp.float32)
    factor = 1.0 / math.sqrt(rows * devices)
    summed = (summed * factor).astype(jnp.bfloat16)
    grad_qkv = jnp.stack([summed[:, :wide], summed[:, wide : 2 * wide]])
    outs = summed[:, 2 * wide :].reshape(own, 2, HEADS * HD)
    return (d_tokens[None], grad_qkv, outs.transpose(1, 2, 0))


def solution(mesh):
    in_specs = (P("rep", "seq", None), P("rep", "seq"), P("rep", "seq", None), P(), P(), P())
    out_specs = (
        P("rep", "seq", None),
        P(None, ("seq", "rep"), None),
        P(None, None, ("seq", "rep")),
    )
    return jax.shard_map(local, mesh=mesh, in_specs=in_specs, out_specs=out_specs, check_vma=False)
```

time: 572 us -> 426 us (0.74)
  waiting for transfers between devices: 368 us -> 283 us
  local copies, waits for them, and re-layouts: 65.1 us -> 39.9 us
  starting transfers between devices: 30.9 us -> 5.98 us
  blocking collectives: 0 us -> 13.2 us
  other arithmetic: 41.9 us -> 29.6 us
  matrix products: 49.3 us -> 37.3 us
    all_to_all x3 -> x1, waiting for transfers between devices: 76 us -> 6.92 us  [exchange(): lax.all_to_all(values, 'seq', split_axis=0, concat_axis=0, tiled=True, ax...]
    another operation x4 -> x1, local copies, waits for them, and re-layouts: 40.3 us -> 0.01 us  [local(): grad_qkv = jnp.stack([summed[:, :wide], summed[:, wide:2 * wide]])]
    all_to_all x3 -> x1, starting transfers between devices: 30.8 us -> 5.94 us  [exchange(): lax.all_to_all(values, 'seq', split_axis=0, concat_axis=0, tiled=True, ax...]
    concatenate x0 -> x2, other arithmetic: none -> 20.4 us  [the longest x1 19.5 us: local(): jnp.concatenate([contract_rows(hidden_s, d_packed_s), contract_rows(hidde...]
    unnamed x2, waiting for transfers between devices: 292 us -> 276 us
    concatenate x0 -> x2, local copies, waits for them, and re-layouts: none -> 14.8 us  [the longest x1 12.7 us: local(): jnp.concatenate([contract_rows(hidden_s, d_packed_s), contract_rows(hidde...]
    another operation x4 -> x1, other arithmetic: 13.6 us -> 0.01 us  [local(): grad_qkv = jnp.stack([summed[:, :wide], summed[:, wide:2 * wide]])]
    convert_element_type x8 -> x6, other arithmetic: 15.7 us -> 2.44 us  [the longest x1 1.22 us: local(): summed = (summed * factor).astype(jnp.bfloat16)]
  transfers between devices with their start and end apart: 4 -> 2, of which waited for: 4 -> 2; matrix products, arithmetic and copies ran while one was open for 4% -> 1% of each run, Pallas kernels for 0% -> 0%
where the time goes in v1:
time: 426 us; the launch traced here: 423 us
  waiting for transfers between devices  283 us (66%)
  local copies, waits for them, and re-layouts  39.9 us (9%)
  matrix products  37.3 us (9%)
  other arithmetic  29.6 us (7%)
  between operations  14.7 us (3%)
  blocking collectives  13.2 us (3%)
  starting transfers between devices  5.98 us (1%)
    unnamed x2, waiting for transfers between devices  276 us
    concatenate x1, other arithmetic, local(): jnp.concatenate([contract_rows(hidden_s, d_packed_s), contract_rows(hidde...  19.5 us
    convert_element_type x1, local copies, waits for them, and re-layouts, local(): sums = jnp.concatenate([contract_rows(hidden_s, d_packed_s), contract_row...  19.2 us
    dot_general x12, matrix products, times_transposed(): lax.dot_general(left, right, (((1,), (1,)), ((), ())), preferred_element_...  13.4 us
    all_to_all x1, blocking collectives, exchange(): lax.all_to_all(values, 'seq', split_axis=0, concat_axis=0, tiled=True, ax...  13.2 us
    dot_general x11, matrix products, dot(): return jnp.dot(left, right, preferred_element_type=jnp.float32)  12.7 us
    concatenate x1, local copies, waits for them, and re-layouts, local(): jnp.concatenate([contract_rows(hidden_s, d_packed_s), contract_rows(hidde...  12.7 us
    dot_general x12, matrix products, contract_rows(): lax.dot_general(left, right, (((0,), (0,)), ((), ())), preferred_element_...  11.2 us
  transfers between devices with their start and end apart: 2, of which 2 were waited for; matrix products, arithmetic and copies ran while one was open for 1% of the time, Pallas kernels for 0%

profile of v1, /device:TPU:1, one launch (start us, length us, event | category | flops | bytes accessed | tf_op | source)
XLA Modules:
  0.0 423.2 jit_solution(12139032898634035896)
XLA Ops:
  7.2 1.6 convert_reduce_fusion
  8.8 1.7 fusion.26
  11.4 3.2 fusion.36
  17.7 1.4 copy-done.3
  21.8 5.9 %all-to-all-start = ((bf16[8,32,1024]{2,1,0:T(8,128)(2,1)}), bf16[8,32,1024]{2,1,0:T(8,128)(2,1)}, u32[]{:S(2)}, u32[]{:S(2)}) async-start(bf16[8,32,1024]{2,1,0:T(8,128)(2,1)} %bitcast.111), calls=%async_computation | async-start | bytes 1048576 | tf_op jit(solution)/shard_map/all_to_all | solution.py:109
  28.4 6.9 %all-to-all-done = bf16[8,32,1024]{2,1,0:T(8,128)(2,1)} async-done(((bf16[8,32,1024]{2,1,0:T(8,128)(2,1)}), bf16[8,32,1024]{2,1,0:T(8,128)(2,1)}, u32[]{:S(2)}, u32[]{:S(2)}) %all-to-all-start) | async-done | bytes 524320 | tf_op jit(solution)/shard_map/all_to_all | solution.py:109
  38.8 1.7 fusion.78
  41.7 1.7 fusion.80
  43.4 1.7 fusion.82
  45.1 1.7 fusion.84
  46.8 1.7 fusion.98
  48.5 1.7 fusion.97
  50.2 1.7 fusion.96
  51.9 1.7 fusion.95
  53.5 2.0 copy.16
  55.6 13.2 %all_to_all.24 = bf16[8,32,1024]{2,1,0:T(8,128)(2,1)S(1)} all-to-all(bf16[8,32,1024]{2,1,0:T(8,128)(2,1)} %bitcast.112), channel_id=1, replica_groups={{0,32,64,96,128,160,192,224},{2,34,66,98,130,162,194,226},{4,36,68,100,..., dimensions={0} | all-to-all | bytes 1048576 | tf_op jit(solution)/shard_map/all_to_all | solution.py:109
  68.8 3.4 fusion.172
  77.0 1.3 convolution_convert_fusion.1
  81.1 19.5 %pad_maximum_fusion = bf16[2304,2048]{0,1:T(8,128)(2,1)} fusion(bf16[2304,256]{0,1:T(8,128)(2,1)S(1)} %convolution_convert_fusion.3, bf16[2304,256]{0,1:T(8,128)(2,1)S(1)} %convolution_convert_fusion.2, bf16[2304,768]{0,1:T(8,128)(2,1)S(1)} %convolution_convert_fusion.1, bf16[2304,768]{0,1:T(8,128)(2,1)S(1)} %convolution_convert_fusion), kind=kLoop, calls=%fused_computation | loop fusion | flops 37748736 | bytes 18874368 | tf_op jit(solution)/shard_map/concatenate | solution.py:134
  100.6 12.7 %copy.17 = bf16[2304,2048]{1,0:T(8,128)(2,1)} copy(bf16[2304,2048]{0,1:T(8,128)(2,1)} %pad_maximum_fusion) | data formatting | bytes 18874368 | tf_op jit(solution)/shard_map/concatenate | solution.py:134
  113.3 19.2 %convert_element_type.159 = bf16[256,18432]{1,0:T(8,128)(2,1)} reshape(bf16[2304,2048]{1,0:T(8,128)(2,1)} %copy.17) | data formatting | bytes 18874368 | tf_op jit(solution)/shard_map/convert_element_type | solution.py:142
  132.6 3.7 fusion.171
  136.3 2.0 fusion.48
  138.3 275.6 %all-reduce.3.cloned.1.call-done = bf16[256,18432]{1,0:T(8,128)(2,1)} async-done(((bf16[256,18432]{1,0:T(8,128)(2,1)}), bf16[256,18432]{1,0:T(8,128)(2,1)}) %all-reduce.3.cloned.1.call-update) | async-done | bytes 9437200
  (139 shorter events, 21.5 us)
Async XLA Ops:
  7.2 4.2 copy-start
  7.2 3.4 copy-start.23
  8.8 2.0 copy-start.30
  10.8 7.0 %copy-start.19 = (f32[2304]{0:T(1024)}, f32[2304]{0:T(1024)S(1)}, u32[]{:S(2)}) copy-start(f32[2304]{0:T(1024)S(1)} %get-tuple-element.18) | copy-start | bytes 27652
  10.8 8.9 %copy-start.15 = (f32[2304]{0:T(1024)}, f32[2304]{0:T(1024)S(1)}, u32[]{:S(2)}) copy-start(f32[2304]{0:T(1024)S(1)} %get-tuple-element.13) | copy-start | bytes 27652
  10.8 8.9 %copy-start.17 = (f32[2304]{0:T(1024)}, f32[2304]{0:T(1024)S(1)}, u32[]{:S(2)}) copy-start(f32[2304]{0:T(1024)S(1)} %get-tuple-element.14) | copy-start | bytes 27652
  11.3 3.3 copy-start.43
  14.6 2.7 copy-start.21
  14.6 2.1 copy-start.9
  15.8 3.9 copy-start.42
  17.3 1.8 copy-start.3
  17.7 3.2 copy-start.24
  21.8 13.5 %all-to-all-start = ((bf16[8,32,1024]{2,1,0:T(8,128)(2,1)}), bf16[8,32,1024]{2,1,0:T(8,128)(2,1)}, u32[]{:S(2)}, u32[]{:S(2)}) async-start(bf16[8,32,1024]{2,1,0:T(8,128)(2,1)} %bitcast.111), calls=%async_computation | async-start | bytes 1048576 | tf_op jit(solution)/shard_map/all_to_all | solution.py:109
  27.8 386.1 %all-reduce.3.cloned.1.call-start = ((), (), s32[]{:S(2)}) async-start(), calls=%async_computation.2 | async-start | bytes 18874368
  68.8 3.4 copy-start.4
  68.8 3.4 copy-start.25
  72.2 1.7 copy-start.10
  73.9 2.6 copy-start.1
  73.9 1.7 copy-start.6
  73.9 1.7 copy-start.33
  73.9 1.7 copy-start.35
  73.9 1.9 copy-start.20
  78.3 1.5 copy-start.27
  132.5 3.7 copy-start.2
  (22 other events, 22.7 us)
Sparse Core Ops, SparseCore 0:
  132.7 281.1 all-reduce.2

commit v2 on v1

--- a/solution.py
+++ b/solution.py
@@ -3,12 +3,15 @@
 import jax
 import jax.numpy as jnp
 from jax import lax
+from jax.experimental import pallas as pl
+from jax.experimental.pallas import tpu as pltpu
 from jax.sharding import PartitionSpec as P
 
 HD = 128
 HEADS = 2
 FRAMES = 8
 epsilon = 1e-06
+MESH = pl.DeviceIdType.MESH
 
 
 def normalize(values):
@@ -89,6 +92,261 @@
     return (
         d_block.astype(jnp.float32) + norm_back(d_hidden * (1.0 + mod_rows[1]), normed, inv_std)
     ).astype(jnp.bfloat16)
+
+
+X_ROWS, Z_ROWS = 64, 16
+BLOCK_ROWS = 288
+OWN = 9
+
+
+def reduce_kernel(t_ref, out_ref, xa, xc, xm, xb, xu, ya, yc, ym, yb, yu,
+                  x2, x2m, x2v, y2, y2m, y2v, tz, zr, zu, zx, zxm, zxv, zy, zym,
+                  last_out, last_in, spread, gather, final,
+                  send_sem, recv_sem):
+    seq = lax.axis_index("seq")
+    x_hi = lax.axis_index("rep")
+    core = lax.rem(seq, 2)
+    z = lax.rem(lax.div(seq, 2), 8)
+    y = lax.rem(lax.div(seq, 16), 4)
+    x_lo = lax.div(seq, 64)
+    x = 2 * x_hi + x_lo
+    bf16, f32 = jnp.bfloat16, jnp.float32
+
+    def device(x_at, y_at, z_at, core_at):
+        return {"seq": ((lax.rem(x_at, 2) * 4 + y_at) * 8 + z_at) * 2 + core_at, "rep": lax.div(x_at, 2)}
+
+    def turn(at, step, size):
+        return lax.rem(at + step + size, size)
+
+    x_right, x_left = device(turn(x, 1, 4), y, z, core), device(turn(x, 3, 4), y, z, core)
+    y_right, y_left = device(x, turn(y, 1, 4), z, core), device(x, turn(y, 3, 4), z, core)
+    z_peers = [device(x, y, turn(z, k, 8), core) for k in range(1, 8)]
+    x_far = turn(x, 2, 4)
+    mates = [device(x, y, z, 1 - core), device(x_far, y, z, core), device(x_far, y, z, 1 - core)]
+
+    barrier = pltpu.get_barrier_semaphore()
+    peers = [x_right, x_left, y_right, y_left] + z_peers + mates
+    for peer in peers:
+        pl.semaphore_signal(barrier, inc=1, device_id=peer, device_id_type=MESH)
+    pl.semaphore_wait(barrier, len(peers))
+
+    used = []
+
+    def send(src, dst, peer):
+        at = len(used)
+        copy = pltpu.make_async_remote_copy(
+            src_ref=src, dst_ref=dst, send_sem=send_sem.at[at], recv_sem=recv_sem.at[at],
+            device_id=peer, device_id_type=MESH,
+        )
+        copy.start()
+        used.append(copy)
+        return copy
+
+    def rows(x_at, y_at, offset, size):
+        start = (lax.rem(x_at, 2) * 4 + y_at) * BLOCK_ROWS + offset + size * lax.div(x_at, 2)
+        return pl.ds(pl.multiple_of(start, 16), size)
+
+    def x_src(a, b):
+        return t_ref.at[rows(a, b, 0, X_ROWS)]
+
+    def y_src(a, b):
+        return t_ref.at[rows(b, a, 2 * X_ROWS, X_ROWS)]
+
+    def far_sends(me, src, box, right, left):
+        far = turn(me, 2, 4)
+        a = [send(src(far, b), box.at[0, b], right) for b in (0, 1)]
+        c = [send(src(far, b), box.at[0, b], left) for b in (2, 3)]
+        return a, c
+
+    def near_sends(me, src, box, right, left):
+        a = [send(src(turn(me, 1, 4), b), box.at[b], right) for b in (2, 3)]
+        c = [send(src(turn(me, 3, 4), b), box.at[b], left) for b in (0, 1)]
+        return a + c
+
+    def relay(me, src, box, mid, into, far, right, left):
+        outs = []
+        for n in range(2):
+            far[0][n].wait_recv()
+            mid[n] = (box[0, n].astype(f32) + src(turn(me, 1, 4), n)[...].astype(f32)).astype(bf16)
+            outs.append(send(mid.at[n], into.at[n], right))
+            far[1][n].wait_recv()
+            mid[n + 2] = (box[0, n + 2].astype(f32) + src(turn(me, 3, 4), n + 2)[...].astype(f32)).astype(bf16)
+            outs.append(send(mid.at[n + 2], into.at[n + 2], left))
+        return outs
+
+    def finish(me, src, near, into, copies, total):
+        for copy in copies:
+            copy.wait_recv()
+        for b in range(4):
+            total[b] = (src(me, b)[...].astype(f32) + near[b].astype(f32) + into[b].astype(f32)).astype(bf16)
+
+    x_far_sends = far_sends(x, x_src, xa, x_right, x_left)
+    y_far_sends = far_sends(y, y_src, ya, y_right, y_left)
+    for u in range(8):
+        for a in range(4):
+            for b in range(4):
+                tz[u, a, b] = t_ref[pl.ds((a % 2 * 4 + b) * BLOCK_ROWS + 4 * X_ROWS + Z_ROWS * (a // 2), Z_ROWS), pl.ds(u * HD, HD)]
+    z_sends = [send(tz.at[turn(z, k, 8)], zr.at[k - 1], z_peers[k - 1]) for k in (4, 3, 5, 2, 6, 1, 7)]
+    x_near = near_sends(x, x_src, xb, x_right, x_left)
+    y_near = near_sends(y, y_src, yb, y_right, y_left)
+    x_relays = relay(x, x_src, xa, xm, xc, x_far_sends, x_right, x_left)
+    y_relays = relay(y, y_src, ya, ym, yc, y_far_sends, y_right, y_left)
+
+    def second_start(me, held, box, right, left):
+        half = X_ROWS // 2
+        far = turn(me, 2, 4)
+        lo, hi = pl.ds(0, half), pl.ds(half, half)
+        return [
+            send(held.at[far, lo], box.at[0, lo], right),
+            send(held.at[far, hi], box.at[0, hi], left),
+            send(held.at[turn(me, 1, 4), hi], box.at[1, hi], right),
+            send(held.at[turn(me, 3, 4), lo], box.at[1, lo], left),
+        ]
+
+    def second_relay(me, held, box, mid, copies, right, left):
+        half = X_ROWS // 2
+        lo, hi = pl.ds(0, half), pl.ds(half, half)
+        copies[0].wait_recv()
+        mid[lo, :] = (box[0, lo, :].astype(f32) + held[turn(me, 1, 4), lo, :].astype(f32)).astype(bf16)
+        one = send(mid.at[lo], box.at[2, lo], right)
+        copies[1].wait_recv()
+        mid[hi, :] = (box[0, hi, :].astype(f32) + held[turn(me, 3, 4), hi, :].astype(f32)).astype(bf16)
+        two = send(mid.at[hi], box.at[2, hi], left)
+        return [one, two]
+
+    def second_finish(me, held, box, copies, offset):
+        for copy in copies:
+            copy.wait_recv()
+        total = (held[me].astype(f32) + box[1].astype(f32) + box[2].astype(f32)).astype(bf16)
+        for u in range(8):
+            last_out[u, pl.ds(offset, X_ROWS), :] = total[:, u * HD : (u + 1) * HD]
+
+    finish(x, x_src, xb, xc, x_near + x_relays, xu)
+    x_second = second_start(y, xu, x2, y_right, y_left)
+    finish(y, y_src, yb, yc, y_near + y_relays, yu)
+    y_second = second_start(x, yu, y2, x_right, x_left)
+    for copy in z_sends:
+        copy.wait_recv()
+    zsum = tz[z].astype(f32)
+    for k in range(7):
+        zsum = zsum + zr[k].astype(f32)
+    zu[...] = zsum.astype(bf16)
+    far, right_at, left_at = turn(x, 2, 4), turn(x, 1, 4), turn(x, 3, 4)
+    lo, hi = pl.ds(0, 2), pl.ds(2, 2)
+    z_first = [
+        send(zu.at[far, lo], zx.at[0, lo], x_right),
+        send(zu.at[far, hi], zx.at[0, hi], x_left),
+        send(zu.at[right_at, hi], zx.at[1, hi], x_right),
+        send(zu.at[left_at, lo], zx.at[1, lo], x_left),
+    ]
+    x_second_more = second_relay(y, xu, x2, x2m, x_second, y_right, y_left)
+    y_second_more = second_relay(x, yu, y2, y2m, y_second, x_right, x_left)
+    z_first[0].wait_recv()
+    zxm[lo] = (zx[0, lo].astype(f32) + zu[right_at, lo].astype(f32)).astype(bf16)
+    z_first.append(send(zxm.at[lo], zx.at[2, lo], x_right))
+    z_first[1].wait_recv()
+    zxm[hi] = (zx[0, hi].astype(f32) + zu[left_at, hi].astype(f32)).astype(bf16)
+    z_first.append(send(zxm.at[hi], zx.at[2, hi], x_left))
+    for copy in z_first[2:]:
+        copy.wait_recv()
+    zxv[...] = (zu[x].astype(f32) + zx[1].astype(f32) + zx[2].astype(f32)).astype(bf16)
+    z_second = [
+        send(zxv.at[turn(y, 2, 4)], zy.at[0], y_right),
+        send(zxv.at[turn(y, 3, 4)], zy.at[1], y_left),
+    ]
+    second_finish(y, xu, x2, x_second[2:] + x_second_more, 0)
+    second_finish(x, yu, y2, y_second[2:] + y_second_more, X_ROWS)
+    last_sends = [
+        send(last_out.at[turn(z, k, 8)], last_in.at[k - 1], z_peers[k - 1]) for k in (4, 3, 5, 2, 6, 1, 7)
+    ]
+    z_second[0].wait_recv()
+    zym[...] = (zy[0].astype(f32) + zxv[turn(y, 1, 4)].astype(f32)).astype(bf16)
+    z_second.append(send(zym, zy.at[2], y_right))
+    for copy in z_second[1:]:
+        copy.wait_recv()
+    z_total = zxv[y].astype(f32) + zy[1].astype(f32) + zy[2].astype(f32)
+    for copy in last_sends:
+        copy.wait_recv()
+    total = last_out[z].astype(f32)
+    for k in range(7):
+        total = total + last_in[k].astype(f32)
+    total = jnp.concatenate([total, z_total], axis=0).astype(bf16)
+
+    slots, held_rows = 8 * 4 * 16, 2 * X_ROWS + Z_ROWS
+    slot = lax.broadcasted_iota(jnp.int32, (slots, held_rows), 0)
+    at = lax.broadcasted_iota(jnp.int32, (slots, held_rows), 1)
+    have = jnp.where(
+        at < X_ROWS, at + X_ROWS * x_hi,
+        jnp.where(at < 2 * X_ROWS, at + X_ROWS + X_ROWS * x_hi, at + 2 * X_ROWS + Z_ROWS * x_hi),
+    )
+    within = lax.bitwise_and(slot, 15)
+    want = lax.shift_right_logical(slot, 4) * OWN + within
+    pick = jnp.where((have == want) & (within < OWN), 1.0, 0.0).astype(bf16)
+    spread[...] = jnp.dot(pick, total, preferred_element_type=f32).astype(bf16).reshape(8, 64, HD)
+    gather_sends = [
+        send(spread.at[turn(z, k, 8)], gather.at[z], z_peers[k - 1]) for k in (4, 3, 5, 2, 6, 1, 7)
+    ]
+    gather[z] = spread[z]
+    for copy in gather_sends:
+        copy.wait_recv()
+    mine = core * 2 + x_hi
+    final_sends = []
+    for n, (mate_core, mate_hi) in enumerate([(1 - core, x_hi), (core, 1 - x_hi), (1 - core, 1 - x_hi)]):
+        place = pl.ds(pl.multiple_of((mate_core * 2 + mate_hi) * 16, 16), 16)
+        final_sends.append(send(gather.at[:, place], final.at[n], mates[n]))
+    for copy in final_sends:
+        copy.wait_recv()
+    place = pl.ds(pl.multiple_of(mine * 16, 16), 16)
+    own = gather[:, place, :].astype(f32) + final[1].astype(f32)
+    other = final[0].astype(f32) + final[2].astype(f32)
+    out_ref[core] = own
+    out_ref[1 - core] = other
+    for copy in used:
+        copy.wait_send()
+
+
+def reduce_scatter(t):
+    bf16 = jnp.bfloat16
+    wide = 8 * HD
+    ring = [
+        pltpu.VMEM((1, 4, X_ROWS, wide), bf16),
+        pltpu.VMEM((4, X_ROWS, wide), bf16),
+        pltpu.VMEM((4, X_ROWS, wide), bf16),
+        pltpu.VMEM((4, X_ROWS, wide), bf16),
+        pltpu.VMEM((4, X_ROWS, wide), bf16),
+    ]
+    second = [
+        pltpu.VMEM((3, X_ROWS, wide), bf16),
+        pltpu.VMEM((X_ROWS, wide), bf16),
+        pltpu.VMEM((X_ROWS, wide), bf16),
+    ]
+    scratch = ring + ring + second + second + [
+        pltpu.VMEM((8, 4, 4, Z_ROWS, HD), bf16),
+        pltpu.VMEM((7, 4, 4, Z_ROWS, HD), bf16),
+        pltpu.VMEM((4, 4, Z_ROWS, HD), bf16),
+        pltpu.VMEM((3, 4, Z_ROWS, HD), bf16),
+        pltpu.VMEM((4, Z_ROWS, HD), bf16),
+        pltpu.VMEM((4, Z_ROWS, HD), bf16),
+        pltpu.VMEM((3, Z_ROWS, HD), bf16),
+        pltpu.VMEM((Z_ROWS, HD), bf16),
+        pltpu.VMEM((8, 2 * X_ROWS, HD), bf16),
+        pltpu.VMEM((7, 2 * X_ROWS, HD), bf16),
+        pltpu.VMEM((8, 64, HD), bf16),
+        pltpu.VMEM((8, 64, HD), bf16),
+        pltpu.VMEM((3, 8, 16, HD), bf16),
+        pltpu.SemaphoreType.DMA((80,)),
+        pltpu.SemaphoreType.DMA((80,)),
+    ]
+    return pl.pallas_call(
+        reduce_kernel,
+        out_shape=jax.ShapeDtypeStruct((2, 8, 16, HD), jnp.float32),
+        in_specs=[pl.BlockSpec(memory_space=pltpu.VMEM)],
+        out_specs=pl.BlockSpec(memory_space=pltpu.VMEM),
+        scratch_shapes=scratch,
+        compiler_params=pltpu.CompilerParams(
+            collective_id=0, has_side_effects=True, vmem_limit_bytes=50 * 2**20
+        ),
+    )(t)
 
 
 def local(tokens, window_ids, cotangent, modulation, w_qkv, w_out):
@@ -131,26 +389,39 @@
     d_packed_s = attend_back(packed_s, probs_s, d_att_s)
     d_tokens = input_side(d_middle, d_packed_s, mod_s, w_qkv[0], normed_s, inv_s)
 
+    core = lax.rem(lax.axis_index("seq"), 2)
+    pairs = [(n, n + 1 - 2 * (n % 2)) for n in range(seq)]
+
+    def sibling(values):
+        return lax.ppermute(values, "seq", pairs)
+
+    def of_head(values, parts, h):
+        heads = values.reshape(rows, parts, HEADS, HD)
+        return jnp.where(h == 0, heads[:, :, 0], heads[:, :, 1]).reshape(rows, parts * HD)
+
+    def pooled(left, right, parts):
+        left2 = jnp.concatenate([left, sibling(left)], axis=0)
+        right2 = jnp.concatenate(
+            [of_head(right, parts, core), sibling(of_head(right, parts, 1 - core))], axis=0
+        )
+        return contract_rows(left2, right2)
+
     sums = jnp.concatenate(
         [
-            contract_rows(hidden_s, d_packed_s),
-            contract_rows(hidden_t, d_packed_t),
-            contract_rows(gated_s, attended_s),
-            contract_rows(gated_t, attended_t),
+            pooled(hidden_s, d_packed_s, 3),
+            pooled(gated_s, attended_s, 1),
+            pooled(hidden_t, d_packed_t, 3),
+            pooled(gated_t, attended_t, 1),
         ],
         axis=1,
     ).astype(jnp.bfloat16)
     devices = seq * lax.axis_size("rep")
-    features, columns = sums.shape
-    own = features // devices
-    summed = lax.psum_scatter(
-        sums.reshape(devices, own * columns), ("seq", "rep"), scatter_dimension=0, tiled=True
-    ).reshape(own, columns).astype(jnp.float32)
     factor = 1.0 / math.sqrt(rows * devices)
-    summed = (summed * factor).astype(jnp.bfloat16)
-    grad_qkv = jnp.stack([summed[:, :wide], summed[:, wide : 2 * wide]])
-    outs = summed[:, 2 * wide :].reshape(own, 2, HEADS * HD)
-    return (d_tokens[None], grad_qkv, outs.transpose(1, 2, 0))
+    summed = (reduce_scatter(sums)[:, :, :OWN] * factor).astype(jnp.bfloat16)
+    summed = summed.reshape(HEADS, 2, 4, OWN, HD)
+    grad_qkv = summed[:, :, :3].transpose(1, 3, 2, 0, 4).reshape(2, OWN, wide)
+    grad_out = summed[:, :, 3].transpose(1, 0, 3, 2).reshape(2, HEADS * HD, OWN)
+    return (d_tokens[None], grad_qkv, grad_out)
 
 
 def solution(mesh):

time: 426 us -> 159 us (0.37)
  waiting for transfers between devices: 283 us -> 13.6 us
  Pallas kernels: 0 us -> 55.5 us
  local copies, waits for them, and re-layouts: 39.9 us -> 10.2 us
  other arithmetic: 29.6 us -> 15.6 us
  blocking collectives: 13.2 us -> 0 us
  between operations: 14.7 us -> 1.52 us
  starting transfers between devices: 5.98 us -> 19.1 us
  matrix products: 37.3 us -> 42 us
    unnamed x2 -> x0, waiting for transfers between devices: 276 us -> none
    pallas_call x0 -> x1, Pallas kernels: none -> 55.5 us  [reduce_scatter(): pl.pallas_call(reduce_kernel, out_shape=jax.ShapeDtypeStruct((2, 8, 16, H...]
    convert_element_type x2 -> x0, local copies, waits for them, and re-layouts: 19.2 us -> none  [the longest x1 19.2 us: local(): sums = jnp.concatenate([contract_rows(hidden_s, d_packed_s), contract_row...]
    concatenate x1 -> x2, other arithmetic: 19.5 us -> 2.51 us  [the longest x1 2.5 us: local(): jnp.concatenate([pooled(hidden_s, d_packed_s, 3), pooled(gated_s, attende...]
    all_to_all x1 -> x0, blocking collectives: 13.2 us -> none  [exchange(): lax.all_to_all(values, 'seq', split_axis=0, concat_axis=0, tiled=True, ax...]
    concatenate x1 -> x0, local copies, waits for them, and re-layouts: 12.7 us -> none  [local(): jnp.concatenate([contract_rows(hidden_s, d_packed_s), contract_rows(hidde...]
    ppermute x0 -> x8, starting transfers between devices: none -> 7.93 us  [sibling(): return lax.ppermute(values, 'seq', pairs)]
    dot_general x12, matrix products: 11.2 us -> 18 us  [contract_rows(): lax.dot_general(left, right, (((0,), (0,)), ((), ())), preferred_element_...]
  transfers between devices with their start and end apart: 2 -> 10, of which waited for: 2 -> 3; matrix products, arithmetic and copies ran while one was open for 1% -> 16% of each run, Pallas kernels for 0% -> 0%
where the time goes in v2:
time: 159 us; the launch traced here: 158 us
  Pallas kernels  55.5 us (35%)
  matrix products  42 us (26%)
  starting transfers between devices  19.1 us (12%)
  other arithmetic  15.6 us (10%)
  waiting for transfers between devices  13.6 us (9%)
  local copies, waits for them, and re-layouts  10.2 us (6%)
    pallas_call x1, Pallas kernels, reduce_scatter(): pl.pallas_call(reduce_kernel, out_shape=jax.ShapeDtypeStruct((2, 8, 16, H...  55.5 us
    dot_general x12, matrix products, contract_rows(): lax.dot_general(left, right, (((0,), (0,)), ((), ())), preferred_element_...  18 us
    dot_general x11, matrix products, dot(): return jnp.dot(left, right, preferred_element_type=jnp.float32)  12.7 us
    all_to_all x2, waiting for transfers between devices, exchange(): lax.all_to_all(values, 'seq', split_axis=0, concat_axis=0, tiled=True, ax...  11.9 us
    dot_general x12, matrix products, times_transposed(): lax.dot_general(left, right, (((1,), (1,)), ((), ())), preferred_element_...  11.3 us
    all_to_all x2, starting transfers between devices, exchange(): lax.all_to_all(values, 'seq', split_axis=0, concat_axis=0, tiled=True, ax...  11.1 us
    ppermute x8, starting transfers between devices, sibling(): return lax.ppermute(values, 'seq', pairs)  7.93 us
  transfers between devices with their start and end apart: 10, of which 3 were waited for; matrix products, arithmetic and copies ran while one was open for 16% of the time, Pallas kernels for 0%

profile of v2, /device:TPU:1, one launch (start us, length us, event | category | flops | bytes accessed | tf_op | source)
XLA Modules:
  0.0 157.6 jit_solution(7523775926062893285)
XLA Ops:
  3.5 1.7 %fusion.26 = f32[256]{0:T(256)S(1)} fusion(bf16[1,256,2304]{2,1,0:T(8,128)(2,1)} %param.6, f32[256]{0:T(256)S(1)} %broadcast_multiply_fusion.5), kind=kLoop, calls=%fused_computation.41 | loop fusion | flops 2359040 | bytes 1181696 | tf_op jit(solution)/shard_map/reduce_sum | solution.py:20
  5.3 3.4 %fusion.48 = bf16[256,768]{1,0:T(8,128)(2,1)S(1)} fusion(bf16[2,2304,768]{2,1,0:T(8,128)(2,1)} %param.10, bf16[1,256,2304]{2,1,0:T(8,128)(2,1)S(1)} %copy-done, f32[2304]{0:T(1024)S(1)} %get-tuple-element.9, f32[2304]{0:T(1024)S(1)} %get-tuple-element.10, f32[256]{0:T(256)S(1)} %add_rsqrt_fusion.1, f32[256]{0:T(256)S(1)} %broadcast_multiply_fusion.5), kind=kOutput, calls=%fused_computation.67 | convolution fusion | flops 909705216 | bytes 5132288 | tf_op jit(solution)/shard_map/dot_general | solution.py:45
  16.0 5.9 %all-to-all-start = ((bf16[8,32,1024]{2,1,0:T(8,128)(2,1)}), bf16[8,32,1024]{2,1,0:T(8,128)(2,1)}, u32[]{:S(2)}, u32[]{:S(2)}) async-start(bf16[8,32,1024]{2,1,0:T(8,128)(2,1)} %bitcast.131), calls=%async_computation | async-start | bytes 1048576 | tf_op jit(solution)/shard_map/all_to_all | solution.py:367
  22.5 7.0 %all-to-all-done = bf16[8,32,1024]{2,1,0:T(8,128)(2,1)} async-done(((bf16[8,32,1024]{2,1,0:T(8,128)(2,1)}), bf16[8,32,1024]{2,1,0:T(8,128)(2,1)}, u32[]{:S(2)}, u32[]{:S(2)}) %all-to-all-start) | async-done | bytes 524320 | tf_op jit(solution)/shard_map/all_to_all | solution.py:367
  34.1 1.7 %fusion.87 = bf16[256,1024]{0,1:T(8,128)(2,1)} fusion(bf16[256,256]{0,1:T(8,128)(2,1)S(1)} %multiply_convert_fusion.3, bf16[256,1024]{1,0:T(8,128)(2,1)} %bitcast.10), kind=kOutput, calls=%fused_computation.108 | convolution fusion | flops 16842752 | bytes 262144 | tf_op jit(solution)/shard_map/dot_general | solution.py:45
  35.9 1.7 %fusion.89 = bf16[256,1024]{0,1:T(8,128)(2,1)} fusion(bf16[256,1024]{0,1:T(8,128)(2,1)} %fusion.87, bf16[256,256]{0,1:T(8,128)(2,1)S(1)} %multiply_convert_fusion.2, bf16[256,1024]{1,0:T(8,128)(2,1)} %bitcast.10), kind=kOutput, calls=%fused_computation.110 | convolution fusion | flops 16842752 | bytes 262144 | tf_op jit(solution)/shard_map/dot_general | solution.py:45
  39.3 1.7 %fusion.93 = bf16[256,1024]{0,1:T(8,128)(2,1)} fusion(bf16[256,1024]{0,1:T(8,128)(2,1)} %fusion.91, bf16[256,256]{0,1:T(8,128)(2,1)S(1)} %multiply_convert_fusion.2, bf16[256,1024]{1,0:T(8,128)(2,1)} %bitcast.10), kind=kOutput, calls=%fused_computation.114 | convolution fusion | flops 16842752 | bytes 262144 | tf_op jit(solution)/shard_map/dot_general | solution.py:33
  41.0 1.7 %fusion.97 = bf16[256,1024]{0,1:T(8,128)(2,1)} fusion(bf16[256,1024]{0,1:T(8,128)(2,1)} %fusion.93, bf16[256,1024]{1,0:T(8,128)(2,1)} %bitcast.10, f32[256,256]{0,1:T(8,128)S(1)} %get-tuple-element.33, f32[256]{0:T(256)S(1)} %fusion.111, f32[256]{0:T(256)S(1)} %get-tuple-element.32), kind=kOutput, calls=%fused_computation.122 | convolution fusion | flops 17006592 | bytes 395264 | tf_op jit(solution)/shard_map/dot_general | solution.py:33
  42.7 1.7 %fusion.96 = bf16[256,1024]{0,1:T(8,128)(2,1)} fusion(bf16[256,1024]{0,1:T(8,128)(2,1)} %fusion.97, bf16[256,1024]{1,0:T(8,128)(2,1)} %bitcast.10, f32[256,256]{0,1:T(8,128)S(1)} %get-tuple-element.37, f32[256]{0:T(256)S(1)} %fusion.113, f32[256]{0:T(256)S(1)} %get-tuple-element.36), kind=kOutput, calls=%fused_computation.120 | convolution fusion | flops 17006592 | bytes 395264 | tf_op jit(solution)/shard_map/dot_general | solution.py:33
  47.7 2.0 %copy.17 = bf16[256,1024]{1,0:T(8,128)(2,1)} copy(bf16[256,1024]{0,1:T(8,128)(2,1)} %fusion.94) | data formatting | bytes 1048576 | tf_op jit(solution)/shard_map/concatenate | solution.py:383
  49.8 5.2 %all-to-all-start.1 = ((bf16[8,32,1024]{2,1,0:T(8,128)(2,1)}), bf16[8,32,1024]{2,1,0:T(8,128)(2,1)}, u32[]{:S(2)}, u32[]{:S(2)}) async-start(bf16[8,32,1024]{2,1,0:T(8,128)(2,1)} %bitcast.130), calls=%async_computation.1 | async-start | bytes 1048576 | tf_op jit(solution)/shard_map/all_to_all | solution.py:367
  55.0 2.4 %collective-permute-start.4 = (bf16[256,2304]{1,0:T(8,128)(2,1)}, bf16[256,2304]{1,0:T(8,128)(2,1)}, u32[]{:S(2)}, u32[]{:S(2)}) collective-permute-start(bf16[256,2304]{1,0:T(8,128)(2,1)} %copy-done.6), channel_id=1, source_target_pairs={{0,2},{2,0},{4,6},{6,4},{8,10},{10,8},{12,14},{14,12},{16,18},{18,... | collective-permute-start | bytes 3538952 | tf_op jit(solution)/shard_map/ppermute | solution.py:396
  57.4 4.9 %all-to-all-done.1 = bf16[8,32,1024]{2,1,0:T(8,128)(2,1)} async-done(((bf16[8,32,1024]{2,1,0:T(8,128)(2,1)}), bf16[8,32,1024]{2,1,0:T(8,128)(2,1)}, u32[]{:S(2)}, u32[]{:S(2)}) %all-to-all-start.1) | async-done | bytes 524320 | tf_op jit(solution)/shard_map/all_to_all | solution.py:367
  62.3 3.4 %fusion.178 = (f32[256]{0:T(256)S(1)}, f32[256]{0:T(256)S(1)}, f32[256,2304]{1,0:T(8,128)S(1)}) fusion(f32[256]{0:T(256)} %copy-done.27, f32[256,2304]{1,0:T(8,128)S(1)} %get-tuple-element.31, f32[256]{0:T(256)S(1)} %broadcast_multiply_fusion.4, f32[2304]{0:T(1024)} %copy-done.22, bf16[2,2304,768]{2,1,0:T(8,128)(2,1)} %param.10, bf16[256,1024]{1,0:T(8,128)(2,1)} %bitcast.12), kind=kOutput, calls=%fused_computation.237 | convolution fusion | flops 909508096 | bytes 8667136 | tf_op jit(solution)/shard_map/dot_general | solution.py:39
  65.8 2.4 %fusion.27 = (bf16[256,2304]{1,0:T(8,128)(2,1)S(1)}, bf16[256,2304]{1,0:T(8,128)(2,1)S(1)}, bf16[256,2304]{1,0:T(8,128)(2,1)}) fusion(f32[2304]{0:T(1024)S(1)} %get-tuple-element.11, f32[256]{0:T(256)S(1)} %get-tuple-element.46, f32[256,2304]{1,0:T(8,128)S(1)} %get-tuple-element.31, f32[256]{0:T(256)S(1)} %broadcast_multiply_fusion.4, ...), kind=kLoop, calls=%fused_computation.42 | loop fusion | flops 8257536 | bytes 9459712 | tf_op jit(solution)/shard_map/convert_element_type | solution.py:87
  73.4 2.5 %fusion.25 = (bf16[256,2304]{1,0:T(8,128)(2,1)}, bf16[1,256,2304]{2,1,0:T(8,128)(2,1)}) fusion(bf16[1,256,2304]{2,1,0:T(8,128)(2,1)S(1)} %copy-done, f32[2304]{0:T(1024)S(1)} %copy-done.24, f32[2304]{0:T(1024)S(1)} %copy-done.26, f32[256]{0:T(256)S(1)} %copy-done.40, f32[256]{0:T(256)S(1)} %copy-done.30, f32[256]{0:T(256)S(1)} %broadcast_multiply_fusion, ...), kind=kLoop, calls=%fused_computation.40 | loop fusion | flops 7667712 | bytes 7100416 | tf_op jit(solution)/shard_map/convert_element_type | solution.py:81
  75.9 3.4 %collective-permute-start = (bf16[256,2304]{1,0:T(8,128)(2,1)}, bf16[256,2304]{1,0:T(8,128)(2,1)}, u32[]{:S(2)}, u32[]{:S(2)}) collective-permute-start(bf16[256,2304]{1,0:T(8,128)(2,1)} %get-tuple-element.15), channel_id=1, source_target_pairs={{0,2},{2,0},{4,6},{6,4},{8,10},{10,8},{12,14},{14,12},{16,18},{18,... | collective-permute-start | bytes 3538952 | tf_op jit(solution)/shard_map/ppermute | solution.py:396
  84.7 1.7 %collective-permute-done.5 = bf16[256,384]{0,1:T(8,128)(2,1)} collective-permute-done((bf16[256,384]{0,1:T(8,128)(2,1)S(1)}, bf16[256,384]{0,1:T(8,128)(2,1)}, u32[]{:S(2)}, u32[]{:S(2)}) %collective-permute-start.5) | collective-permute-done | bytes 196640 | tf_op jit(solution)/shard_map/ppermute | solution.py:396
  87.0 3.1 %convolution_convert_fusion = bf16[2304,384]{1,0:T(8,128)(2,1)S(1)} fusion(bf16[256,2304]{1,0:T(8,128)(2,1)} %collective-permute-done.4, bf16[256,2304]{1,0:T(8,128)(2,1)} %copy-done.6, bf16[256,384]{0,1:T(8,128)(2,1)} %collective-permute-done.5, bf16[256,384]{0,1:T(8,128)(2,1)S(1)} %bitcast.139), kind=kOutput, calls=%fused_computation.1 | convolution fusion | flops 912359424 | bytes 4521984 | tf_op jit(solution)/shard_map/dot_general | solution.py:33
  90.8 3.1 %convolution_convert_fusion.1 = bf16[2304,384]{1,0:T(8,128)(2,1)S(1)} fusion(bf16[256,2304]{1,0:T(8,128)(2,1)} %collective-permute-done, bf16[256,2304]{1,0:T(8,128)(2,1)} %get-tuple-element.15, bf16[256,384]{0,1:T(8,128)(2,1)S(1)} %collective-permute-done.1, bf16[256,384]{0,1:T(8,128)(2,1)S(1)} %bitcast.138), kind=kOutput, calls=%fused_computation.2 | convolution fusion | flops 912359424 | bytes 4521984 | tf_op jit(solution)/shard_map/dot_general | solution.py:33
  93.9 2.1 %convolution_convert_fusion.3 = bf16[2304,128]{1,0:T(8,128)(2,1)S(1)} fusion(bf16[256,2304]{1,0:T(8,128)(2,1)} %collective-permute-done.2, bf16[256,2304]{1,0:T(8,128)(2,1)S(1)} %copy-done.5, bf16[256,128]{0,1:T(8,128)(2,1)S(1)} %collective-permute-done.3, bf16[256,128]{0,1:T(8,128)(2,1)S(1)} %copy-done.19), kind=kOutput, calls=%fused_computation.10 | convolution fusion | flops 307265536 | bytes 3080192 | tf_op jit(solution)/shard_map/dot_general | solution.py:33
  96.0 2.1 %convolution_convert_fusion.2 = bf16[2304,128]{1,0:T(8,128)(2,1)S(1)} fusion(bf16[256,2304]{1,0:T(8,128)(2,1)} %collective-permute-done.6, bf16[256,2304]{1,0:T(8,128)(2,1)S(1)} %copy-done.3, bf16[256,128]{0,1:T(8,128)(2,1)S(1)} %collective-permute-done.7, bf16[256,128]{0,1:T(8,128)(2,1)S(1)} %get-tuple-element.24), kind=kOutput, calls=%fused_computation.9 | convolution fusion | flops 307265536 | bytes 3080192 | tf_op jit(solution)/shard_map/dot_general | solution.py:33
  98.1 2.5 %pad_maximum_fusion.t_ref = bf16[2304,1024]{1,0:T(8,128)(2,1)} fusion(bf16[2304,128]{1,0:T(8,128)(2,1)S(1)} %convolution_convert_fusion.2, bf16[2304,384]{1,0:T(8,128)(2,1)S(1)} %convolution_convert_fusion, bf16[2304,128]{1,0:T(8,128)(2,1)S(1)} %convolution_convert_fusion.3, bf16[2304,384]{1,0:T(8,128)(2,1)S(1)} %convolution_convert_fusion.1), kind=kLoop, calls=%fused_computation | loop fusion | flops 18874368 | bytes 9437184 | tf_op jit(solution)/shard_map/concatenate | solution.py:409
  100.6 55.5 %shard_map.85 = f32[2,8,16,128]{3,2,1,0:T(8,128)S(1)} custom-call(bf16[2304,1024]{1,0:T(8,128)(2,1)} %pad_maximum_fusion.t_ref), custom_call_target="tpu_custom_call" | custom-call | tf_op jit(solution)/shard_map/pallas_call | solution.py:340
  (168 shorter events, 33.1 us)
Async XLA Ops:
  0.6 4.7 %copy-start = (bf16[1,256,2304]{2,1,0:T(8,128)(2,1)S(1)}, bf16[1,256,2304]{2,1,0:T(8,128)(2,1)}, u32[]{:S(2)}) copy-start(bf16[1,256,2304]{2,1,0:T(8,128)(2,1)} %param.6) | copy-start | bytes 3538948
  2.0 6.7 %copy-start.23 = (f32[2304]{0:T(1024)}, f32[2304]{0:T(1024)S(1)}, u32[]{:S(2)}) copy-start(f32[2304]{0:T(1024)S(1)} %get-tuple-element.9) | copy-start | bytes 27652
  2.0 6.7 %copy-start.25 = (f32[2304]{0:T(1024)}, f32[2304]{0:T(1024)S(1)}, u32[]{:S(2)}) copy-start(f32[2304]{0:T(1024)S(1)} %get-tuple-element.10) | copy-start | bytes 27652
  2.0 9.9 %copy-start.22 = (f32[2304]{0:T(1024)}, f32[2304]{0:T(1024)S(1)}, u32[]{:S(2)}) copy-start(f32[2304]{0:T(1024)S(1)} %get-tuple-element.8) | copy-start | bytes 27652
  2.0 12.1 %copy-start.20 = (f32[2304]{0:T(1024)}, f32[2304]{0:T(1024)S(1)}, u32[]{:S(2)}) copy-start(f32[2304]{0:T(1024)S(1)} %get-tuple-element.12) | copy-start | bytes 27652
  3.5 5.2 %copy-start.29 = (f32[256]{0:T(256)}, f32[256]{0:T(256)S(1)}, u32[]{:S(2)}) copy-start(f32[256]{0:T(256)S(1)} %broadcast_multiply_fusion.5) | copy-start | bytes 3076
  5.3 3.5 %copy-start.39 = (f32[256]{0:T(256)}, f32[256]{0:T(256)S(1)}, u32[]{:S(2)}) copy-start(f32[256]{0:T(256)S(1)} %add_rsqrt_fusion.1) | copy-start | bytes 3076
  5.3 3.5 %copy-start.41 = (s32[1,256]{1,0:T(1,128)S(1)}, s32[1,256]{1,0:T(1,128)}, u32[]{:S(2)}) copy-start(s32[1,256]{1,0:T(1,128)} %param.7) | copy-start | bytes 3076
  5.3 7.6 %slice-start = ((s8[7077888]{0:T(1024)(128)(4,1)}), s8[4194304]{0:T(1024)(128)(4,1)S(1)}, s32[]{:S(2)}) async-start(s8[7077888]{0:T(1024)(128)(4,1)} %bitcast.142), calls=%async_computation.2 | async-start | bytes 8388608
  16.0 13.5 %all-to-all-start = ((bf16[8,32,1024]{2,1,0:T(8,128)(2,1)}), bf16[8,32,1024]{2,1,0:T(8,128)(2,1)}, u32[]{:S(2)}, u32[]{:S(2)}) async-start(bf16[8,32,1024]{2,1,0:T(8,128)(2,1)} %bitcast.131), calls=%async_computation | async-start | bytes 1048576 | tf_op jit(solution)/shard_map/all_to_all | solution.py:367
  49.8 12.5 %all-to-all-start.1 = ((bf16[8,32,1024]{2,1,0:T(8,128)(2,1)}), bf16[8,32,1024]{2,1,0:T(8,128)(2,1)}, u32[]{:S(2)}, u32[]{:S(2)}) async-start(bf16[8,32,1024]{2,1,0:T(8,128)(2,1)} %bitcast.130), calls=%async_computation.1 | async-start | bytes 1048576 | tf_op jit(solution)/shard_map/all_to_all | solution.py:367
  55.0 31.8 %collective-permute-start.4 = (bf16[256,2304]{1,0:T(8,128)(2,1)}, bf16[256,2304]{1,0:T(8,128)(2,1)}, u32[]{:S(2)}, u32[]{:S(2)}) collective-permute-start(bf16[256,2304]{1,0:T(8,128)(2,1)} %copy-done.6), channel_id=1, source_target_pairs={{0,2},{2,0},{4,6},{6,4},{8,10},{10,8},{12,14},{14,12},{16,18},{18,... | collective-permute-start | bytes 3538952 | tf_op jit(solution)/shard_map/ppermute | solution.py:396
  65.7 5.9 %slice-start.2 = ((s8[7077888]{0:T(1024)(128)(4,1)}), s8[2883584]{0:T(1024)(128)(4,1)S(1)}, s32[]{:S(2)}) async-start(s8[7077888]{0:T(1024)(128)(4,1)} %bitcast.144), calls=%async_computation.4 | async-start | bytes 5767168
  73.4 6.0 %copy-start.14 = (bf16[256,128]{0,1:T(8,128)(2,1)S(1)}, bf16[256,128]{0,1:T(8,128)(2,1)}, u32[]{:S(2)}) copy-start(bf16[256,128]{0,1:T(8,128)(2,1)} %copy-done.13) | copy-start | bytes 196612
  73.4 6.0 %copy-start.16 = (bf16[256,128]{0,1:T(8,128)(2,1)S(1)}, bf16[256,128]{0,1:T(8,128)(2,1)}, u32[]{:S(2)}) copy-start(bf16[256,128]{0,1:T(8,128)(2,1)} %copy-done.15) | copy-start | bytes 196612
  73.4 6.0 %copy-start.5 = (bf16[256,2304]{1,0:T(8,128)(2,1)S(1)}, bf16[256,2304]{1,0:T(8,128)(2,1)}, u32[]{:S(2)}) copy-start(bf16[256,2304]{1,0:T(8,128)(2,1)} %copy-done.4) | copy-start | bytes 3538948
  75.9 7.0 %copy-start.3 = (bf16[256,2304]{1,0:T(8,128)(2,1)S(1)}, bf16[256,2304]{1,0:T(8,128)(2,1)}, u32[]{:S(2)}) copy-start(bf16[256,2304]{1,0:T(8,128)(2,1)} %get-tuple-element.17) | copy-start | bytes 3538948
  75.9 14.9 %collective-permute-start = (bf16[256,2304]{1,0:T(8,128)(2,1)}, bf16[256,2304]{1,0:T(8,128)(2,1)}, u32[]{:S(2)}, u32[]{:S(2)}) collective-permute-start(bf16[256,2304]{1,0:T(8,128)(2,1)} %get-tuple-element.15), channel_id=1, source_target_pairs={{0,2},{2,0},{4,6},{6,4},{8,10},{10,8},{12,14},{14,12},{16,18},{18,... | collective-permute-start | bytes 3538952 | tf_op jit(solution)/shard_map/ppermute | solution.py:396
  79.4 14.5 %collective-permute-start.2 = (bf16[256,2304]{1,0:T(8,128)(2,1)S(1)}, bf16[256,2304]{1,0:T(8,128)(2,1)}, u32[]{:S(2)}, u32[]{:S(2)}) collective-permute-start(bf16[256,2304]{1,0:T(8,128)(2,1)S(1)} %copy-done.5), channel_id=1, source_target_pairs={{0,2},{2,0},{4,6},{6,4},{8,10},{10,8},{12,14},{14,12},{16,18},{18,... | collective-permute-start | bytes 3538952 | tf_op jit(solution)/shard_map/ppermute | solution.py:396
  82.9 13.1 %collective-permute-start.6 = (bf16[256,2304]{1,0:T(8,128)(2,1)S(1)}, bf16[256,2304]{1,0:T(8,128)(2,1)}, u32[]{:S(2)}, u32[]{:S(2)}) collective-permute-start(bf16[256,2304]{1,0:T(8,128)(2,1)S(1)} %copy-done.3), channel_id=1, source_target_pairs={{0,2},{2,0},{4,6},{6,4},{8,10},{10,8},{12,14},{14,12},{16,18},{18,... | collective-permute-start | bytes 3538952 | tf_op jit(solution)/shard_map/ppermute | solution.py:396
  83.5 2.9 %collective-permute-start.5 = (bf16[256,384]{0,1:T(8,128)(2,1)S(1)}, bf16[256,384]{0,1:T(8,128)(2,1)}, u32[]{:S(2)}, u32[]{:S(2)}) collective-permute-start(bf16[256,384]{0,1:T(8,128)(2,1)S(1)} %bitcast.141), channel_id=1, source_target_pairs={{0,2},{2,0},{4,6},{6,4},{8,10},{10,8},{12,14},{14,12},{16,18},{18,... | collective-permute-start | bytes 589832 | tf_op jit(solution)/shard_map/ppermute | solution.py:396
  86.4 3.7 %collective-permute-start.1 = (bf16[256,384]{0,1:T(8,128)(2,1)S(1)}, bf16[256,384]{0,1:T(8,128)(2,1)S(1)}, u32[]{:S(2)}, u32[]{:S(2)}) collective-permute-start(bf16[256,384]{0,1:T(8,128)(2,1)S(1)} %bitcast.140), channel_id=1, source_target_pairs={{0,2},{2,0},{4,6},{6,4},{8,10},{10,8},{12,14},{14,12},{16,18},{18,... | collective-permute-start | bytes 589832 | tf_op jit(solution)/shard_map/ppermute | solution.py:396
  86.8 7.1 %collective-permute-start.3 = (bf16[256,128]{0,1:T(8,128)(2,1)}, bf16[256,128]{0,1:T(8,128)(2,1)S(1)}, u32[]{:S(2)}, u32[]{:S(2)}) collective-permute-start(bf16[256,128]{0,1:T(8,128)(2,1)} %get-tuple-element.23), channel_id=1, source_target_pairs={{0,2},{2,0},{4,6},{6,4},{8,10},{10,8},{12,14},{14,12},{16,18},{18,... | collective-permute-start | bytes 196616 | tf_op jit(solution)/shard_map/ppermute | solution.py:396
  90.1 5.9 %collective-permute-start.7 = (bf16[256,128]{0,1:T(8,128)(2,1)S(1)}, bf16[256,128]{0,1:T(8,128)(2,1)S(1)}, u32[]{:S(2)}, u32[]{:S(2)}) collective-permute-start(bf16[256,128]{0,1:T(8,128)(2,1)S(1)} %get-tuple-element.25), channel_id=1, source_target_pairs={{0,2},{2,0},{4,6},{6,4},{8,10},{10,8},{12,14},{14,12},{16,18},{18,... | collective-permute-start | bytes 196616 | tf_op jit(solution)/shard_map/ppermute | solution.py:396
  (32 other events, 61.3 us)

commit v3 on v1

v3 whole, which is shorter than its diff:
```python
import math

import jax
import jax.numpy as jnp
from jax import lax
from jax.experimental import pallas as pl
from jax.experimental.pallas import tpu as pltpu
from jax.sharding import PartitionSpec as P

MESH = pl.DeviceIdType.MESH
BF16, F32 = jnp.bfloat16, jnp.float32
HD = 128
HEADS = 2
FRAMES = 8
UNITS = 4
WIDE = UNITS * HD
BLOCK_ROWS = 288
X_ROWS, Z_ROWS = 64, 16
OWN = 9
SLOT = 16
epsilon = 1e-06
factor_of_scores = HD ** (-0.5)


def nn(left, right):
    return lax.dot_general(left, right, (((1,), (0,)), ((), ())), preferred_element_type=F32)


def nt(left, right):
    return lax.dot_general(left, right, (((1,), (1,)), ((), ())), preferred_element_type=F32)


def softmax(query, key, mask):
    scores = jnp.where(mask, nt(query, key) * factor_of_scores, -1e30)
    expd = jnp.exp(scores - jnp.max(scores, axis=-1, keepdims=True))
    return expd / jnp.sum(expd, axis=-1, keepdims=True)


def attend_back(query, key, value, probs, d_out):
    d_value = nn(probs.astype(BF16).T, d_out)
    d_prob = nt(d_out, value)
    d_score = (probs * (d_prob - jnp.sum(probs * d_prob, axis=-1, keepdims=True))).astype(BF16)
    d_query = nn(d_score, key) * factor_of_scores
    d_key = nn(d_score.T, query) * factor_of_scores
    return d_query.astype(BF16), d_key.astype(BF16), d_value.astype(BF16)


def normalize(values):
    centered = values - jnp.mean(values, axis=-1, keepdims=True)
    inv_std = lax.rsqrt(jnp.mean(centered * centered, axis=-1, keepdims=True) + epsilon)
    return centered * inv_std, inv_std


def norm_back(d_normed, normed, inv_std):
    return inv_std * (
        d_normed
        - jnp.mean(d_normed, axis=-1, keepdims=True)
        - normed * jnp.mean(d_normed * normed, axis=-1, keepdims=True)
    )


def whole_kernel(tokens_hbm, ids_ref, cot_hbm, mod_ref, qkv_hbm, out_hbm,
                 grad_ref, sums_ref,
                 x_ref, cot_ref, w0, w1, wo0, wo1,
                 hid0, hid1, mid, g1, g0, acc, pk0, probs, att0,
                 ht0, ht1, gt0, gt1, sib_ht0, sib_ht1, sib_gt0, sib_gt1,
                 out_s, in_s, out_p, back, dp, b0, sib_b1, sib_b0,
                 *rest):
    per_block = 22
    boxes = [rest[:per_block], rest[per_block : 2 * per_block]]
    spread, gather, merged, final, load_sem, send_sem, recv_sem = rest[2 * per_block :]

    seq = lax.axis_index("seq")
    x_hi = lax.axis_index("rep")
    core = lax.rem(seq, 2)
    z = lax.rem(lax.div(seq, 2), 8)
    y = lax.rem(lax.div(seq, 16), 4)
    x_lo = lax.div(seq, 64)
    x = 2 * x_hi + x_lo
    frame = x_lo * 4 + y

    loads = []
    for n, (src, dst) in enumerate([
        (tokens_hbm.at[0], x_ref), (qkv_hbm.at[0], w0), (out_hbm.at[0], wo0),
        (cot_hbm.at[0], cot_ref), (out_hbm.at[1], wo1), (qkv_hbm.at[1], w1),
    ]):
        loads.append(pltpu.make_async_copy(src, dst, load_sem.at[n]))
        loads[n].start()

    def device(x_at, y_at, z_at, core_at):
        return {"seq": ((lax.rem(x_at, 2) * 4 + y_at) * 8 + z_at) * 2 + core_at, "rep": lax.div(x_at, 2)}

    def turn(at, step, size):
        return lax.rem(at + step, size)

    x_right, x_left = device(turn(x, 1, 4), y, z, core), device(turn(x, 3, 4), y, z, core)
    x_far_at = turn(x, 2, 4)
    z_order = (4, 3, 5, 2, 6, 1, 7)
    z_peers = {k: device(x, y, turn(z, k, 8), core) for k in z_order}
    mates = [device(x, y, z, 1 - core), device(x_far_at, y, z, core), device(x_far_at, y, z, 1 - core)]
    sibling, x_far = mates[0], mates[1]
    other = 2 * x_hi + 1 - x_lo
    clip = []
    for cross, step in ((1, 2), (1, 1), (1, 3), (1, 0), (0, 2), (0, 1), (0, 3)):
        y_at = turn(y, step, 4)
        frame_at = (1 - x_lo if cross else x_lo) * 4 + y_at
        clip.append((frame_at, device(other if cross else x, y_at, z, core)))
    y_far, y_right, y_left = clip[4][1], clip[5][1], clip[6][1]

    barrier = pltpu.get_barrier_semaphore()
    peers = [x_right, x_left] + mates + list(z_peers.values()) + [peer for _, peer in clip]
    for peer in peers:
        pl.semaphore_signal(barrier, inc=1, device_id=peer, device_id_type=MESH)

    used = []

    def send(src, dst, peer):
        at = len(used)
        copy = pltpu.make_async_remote_copy(
            src_ref=src, dst_ref=dst, send_sem=send_sem.at[at], recv_sem=recv_sem.at[at],
            device_id=peer, device_id_type=MESH,
        )
        copy.start()
        used.append(copy)
        return copy

    def arrived(copies):
        for copy in copies:
            copy.wait_recv()

    rows_of = x_ref.shape[0]
    features = x_ref.shape[1]
    shift0, scale0, gate0, shift1, scale1, gate1 = range(6)

    def mod(n):
        return mod_ref[n : n + 1, :]

    def by_rows(body):
        def step(i, carry):
            body(pl.ds(pl.multiple_of(i * 16, 16), 16))
            return carry

        lax.fori_loop(0, rows_of // 16, step, 0)

    def by_columns(body, size=256):
        def step(i, carry):
            body(pl.ds(pl.multiple_of(i * size, size), size))
            return carry

        lax.fori_loop(0, features // size, step, 0)

    loads[0].wait()

    def spatial_in(at):
        normed, _ = normalize(x_ref[at, :].astype(F32))
        hid0[at, :] = (normed * (1.0 + mod(scale0)) + mod(shift0)).astype(BF16)

    by_rows(spatial_in)
    loads[1].wait()

    def project0(i, carry):
        at = pl.ds(pl.multiple_of(i * 256, 256), 256)
        pk0[:, at] = nn(hid0[...], w0[:, at]).astype(BF16)
        return carry

    lax.fori_loop(0, 3, project0, 0)

    ids = jnp.broadcast_to(ids_ref[...], (rows_of, rows_of))
    mask = ids == ids.T

    def part(n, h):
        return pk0[:, (2 * n + h) * HD : (2 * n + h + 1) * HD]

    for h in range(HEADS):
        p = softmax(part(0, h), part(1, h), mask)
        probs[h] = p
        att = nn(p.astype(BF16), part(2, h)).astype(BF16)
        att0[:, h * HD : (h + 1) * HD] = att
        b0[h, :, 3 * HD :] = att
    loads[2].wait()

    def middle(at):
        mid[:, at] = (
            x_ref[:, at].astype(F32) + mod_ref[gate0 : gate0 + 1, at] * nn(att0[...], wo0[:, at])
        ).astype(BF16)

    by_columns(middle)

    def temporal_in(at):
        normed, _ = normalize(mid[at, :].astype(F32))
        hid1[at, :] = (normed * (1.0 + mod(scale1)) + mod(shift1)).astype(BF16)

    by_rows(temporal_in)
    loads[3].wait()

    def gate_top(at):
        g1[at, :] = (mod(gate1) * cot_ref[at, :].astype(F32)).astype(BF16)

    by_rows(gate_top)
    loads[4].wait()
    d_att1 = nt(g1[...], wo1[...]).astype(BF16)
    for h in range(HEADS):
        out_s[h, :, 3 * HD :] = d_att1[:, h * HD : (h + 1) * HD]
    loads[5].wait()

    def project1(i, carry):
        packed = nn(hid1[...], w1[:, pl.ds(pl.multiple_of(i * 256, 256), 256)]).astype(BF16)
        at = pl.ds(pl.multiple_of(i * HD, HD), HD)
        for h in range(HEADS):
            out_s[h, :, at] = packed[:, h * HD : (h + 1) * HD]
        return carry

    lax.fori_loop(0, 3, project1, 0)

    pixels = rows_of // FRAMES

    def pixel_rows(n):
        return pl.ds(pl.multiple_of(n * pixels, pixels), pixels)

    pl.semaphore_wait(barrier, len(peers))
    gone = [
        [send(out_s.at[h, pixel_rows(at)], in_s.at[h, frame], peer) for at, peer in clip]
        for h in range(HEADS)
    ]

    def flip(src, dst):
        def body(at):
            dst[at, :] = src[:, at].T

        by_columns(body)

    flip(hid1, ht1)
    shared1 = [send(ht1, sib_ht1, sibling)]
    flip(g1, gt1)
    shared1.append(send(gt1, sib_gt1, sibling))

    pixel_row = lax.bitwise_and(lax.broadcasted_iota(jnp.int32, (rows_of, rows_of), 0), pixels - 1)
    pixel_col = lax.bitwise_and(lax.broadcasted_iota(jnp.int32, (rows_of, rows_of), 1), pixels - 1)
    same_pixel = pixel_row == pixel_col
    came = []
    for h in range(HEADS):
        in_s[h, frame] = out_s[h, pixel_rows(frame), :]
        arrived(gone[h])
        block = in_s[h].reshape(rows_of, WIDE)
        query, key, value, d_out = [block[:, n * HD : (n + 1) * HD] for n in range(UNITS)]
        p = softmax(query, key, same_pixel)
        out_p[h, :, 3 * HD :] = nn(p.astype(BF16), value).astype(BF16)
        for n, part_of in enumerate(attend_back(query, key, value, p, d_out)):
            out_p[h, :, n * HD : (n + 1) * HD] = part_of
        came.append([
            send(out_p.at[h, pixel_rows(at)], back.at[h, pixel_rows(frame)], peer) for at, peer in clip
        ])
    flip(hid0, ht0)
    shared0 = [send(ht0, sib_ht0, sibling)]
    for h in range(HEADS):
        back[h, pixel_rows(frame), :] = out_p[h, pixel_rows(frame), :]
        arrived(came[h])
    shared1.append(send(back.at[1 - core], sib_b1, sibling))

    def reduction(box, t):
        (_, xa, xc, xm, xb, xu, ya, yc, ym, yb, yu, x2, x2m, y2, y2m, tz, zr, zu, zx, zy, last_out, last_in) = box

        def rows(x_at, y_at, offset):
            start = (lax.rem(x_at, 2) * 4 + y_at) * BLOCK_ROWS + offset + X_ROWS * lax.div(x_at, 2)
            return pl.ds(pl.multiple_of(start, 16), X_ROWS)

        def x_src(a, b):
            return t.at[rows(a, b, 0)]

        def y_src(a, b):
            return t.at[rows(b, a, 2 * X_ROWS)]

        def total2(one, two):
            return (one.astype(F32) + two.astype(F32)).astype(BF16)

        def far_sends(me, src, into, right, left):
            far = turn(me, 2, 4)
            return (
                [send(src(far, b), into.at[b], right) for b in (0, 1)]
                + [send(src(far, b), into.at[b], left) for b in (2, 3)]
            )

        def near_sends(me, src, into, right, left):
            return (
                [send(src(turn(me, 1, 4), b), into.at[b], right) for b in (2, 3)]
                + [send(src(turn(me, 3, 4), b), into.at[b], left) for b in (0, 1)]
            )

        def relay(me, src, box_in, kept, into, far, right, left):
            outs = []
            for n in (0, 2, 1, 3):
                far[n].wait_recv()
                kept[n] = total2(box_in[n], src(turn(me, 1 if n < 2 else 3, 4), n)[...])
                outs.append(send(kept.at[n], into.at[n], right if n < 2 else left))
            return outs

        def finish(me, src, near, into, copies, result):
            arrived(copies)
            for b in range(4):
                result[b] = (
                    src(me, b)[...].astype(F32) + near[b].astype(F32) + into[b].astype(F32)
                ).astype(BF16)

        half = X_ROWS // 2
        lo, hi = pl.ds(0, half), pl.ds(half, half)

        def second_start(me, held, into, right, left):
            far = turn(me, 2, 4)
            return [
                send(held.at[far, lo], into.at[0, lo], right),
                send(held.at[far, hi], into.at[0, hi], left),
                send(held.at[turn(me, 1, 4), hi], into.at[1, hi], right),
                send(held.at[turn(me, 3, 4), lo], into.at[1, lo], left),
            ]

        def second_relay(me, held, into, kept, copies, right, left):
            copies[0].wait_recv()
            kept[lo, :] = total2(into[0, lo, :], held[turn(me, 1, 4), lo, :])
            one = send(kept.at[lo], into.at[2, lo], right)
            copies[1].wait_recv()
            kept[hi, :] = total2(into[0, hi, :], held[turn(me, 3, 4), hi, :])
            return [one, send(kept.at[hi], into.at[2, hi], left)]

        def second_finish(me, held, into, copies, offset):
            arrived(copies)
            total = (held[me].astype(F32) + into[1].astype(F32) + into[2].astype(F32)).astype(BF16)
            for u in range(UNITS):
                for hf in range(2):
                    last_out[2 * u + hf, offset : offset + half, :] = total[
                        hf * half : (hf + 1) * half, u * HD : (u + 1) * HD
                    ]

        def start():
            x_far_sends = far_sends(x, x_src, xa, x_right, x_left)
            y_far_sends = far_sends(y, y_src, ya, y_right, y_left)
            x_near = near_sends(x, x_src, xb, x_right, x_left)
            y_near = near_sends(y, y_src, yb, y_right, y_left)
            for u in range(UNITS):
                for hf in range(2):
                    for a in range(8):
                        top = a * BLOCK_ROWS + 4 * X_ROWS + Z_ROWS * hf
                        tz[2 * u + hf, a] = t[top : top + Z_ROWS, u * HD : (u + 1) * HD]
            z_sends = [send(tz.at[turn(z, k, 8)], zr.at[k - 1], z_peers[k]) for k in z_order]
            yield
            x_relays = relay(x, x_src, xa, xm, xc, x_far_sends, x_right, x_left)
            y_relays = relay(y, y_src, ya, ym, yc, y_far_sends, y_right, y_left)
            yield
            finish(x, x_src, xb, xc, x_near + x_relays, xu)
            x_second = second_start(y, xu, x2, y_right, y_left)
            finish(y, y_src, yb, yc, y_near + y_relays, yu)
            y_second = second_start(x, yu, y2, x_right, x_left)
            arrived(z_sends)
            total = tz[z].astype(F32)
            for k in range(7):
                total = total + zr[k].astype(F32)
            zu[...] = total.astype(BF16)

            def quad(x_lo_at):
                return pl.ds(pl.multiple_of(x_lo_at * 4, 4), 4)

            z_first = [
                send(zu.at[quad(x_lo)], zx.at[0], x_far),
                send(zu.at[quad(1 - x_lo)], zx.at[1], x_right),
                send(zu.at[quad(1 - x_lo)], zx.at[2], x_left),
            ]
            yield
            x_more = second_relay(y, xu, x2, x2m, x_second, y_right, y_left)
            y_more = second_relay(x, yu, y2, y2m, y_second, x_right, x_left)
            arrived(z_first)
            total = zu[quad(x_lo)].astype(F32)
            for n in range(3):
                total = total + zx[n].astype(F32)
            zx[3] = total.astype(BF16)
            z_second = [
                send(zx.at[3, turn(y, 2, 4)], zy.at[0], y_far),
                send(zx.at[3, turn(y, 1, 4)], zy.at[1], y_right),
                send(zx.at[3, turn(y, 3, 4)], zy.at[2], y_left),
            ]
            yield
            second_finish(y, xu, x2, x_second[2:] + x_more, 0)
            second_finish(x, yu, y2, y_second[2:] + y_more, half)
            last = [send(last_out.at[turn(z, k, 8)], last_in.at[k - 1], z_peers[k]) for k in z_order]
            arrived(z_second)
            z_total = zx[3, y].astype(F32)
            for n in range(3):
                z_total = z_total + zy[n].astype(F32)
            yield
            arrived(last)
            total = last_out[z].astype(F32)
            for k in range(7):
                total = total + last_in[k].astype(F32)
            yield jnp.concatenate([total, z_total], axis=0).astype(BF16)

        return start()

    def weight_sums(t, ht, gt, mine, sib_ht, sib_gt, theirs):
        head_qkv, head_att = pl.ds(0, 3 * HD), pl.ds(3 * HD, HD)

        def body(i, carry):
            at = pl.ds(pl.multiple_of(i * BLOCK_ROWS, BLOCK_ROWS), BLOCK_ROWS)
            t[at, head_qkv] = (
                nn(ht[at, :], mine[core, :, head_qkv]) + nn(sib_ht[at, :], theirs[:, head_qkv])
            ).astype(BF16)
            t[at, head_att] = (
                nn(gt[at, :], mine[core, :, head_att]) + nn(sib_gt[at, :], theirs[:, head_att])
            ).astype(BF16)
            return carry

        lax.fori_loop(0, features // BLOCK_ROWS, body, 0)

    def gather_heads(src):
        for n in range(3):
            for h in range(HEADS):
                dp[:, (2 * n + h) * HD : (2 * n + h + 1) * HD] = src[h, :, n * HD : (n + 1) * HD]

    gather_heads(back)

    def input_back(weight):
        def body(at):
            acc[:, at] = nt(dp[...], weight[at, :])

        by_columns(body)

    input_back(w1)
    t1, t0 = boxes[1][0], boxes[0][0]
    arrived(shared1)
    weight_sums(t1, ht1, gt1, back, sib_ht1, sib_gt1, sib_b1)
    steps1 = reduction(boxes[1], t1)
    next(steps1)

    def temporal_back(at):
        normed, inv_std = normalize(mid[at, :].astype(F32))
        term = norm_back(acc[at, :] * (1.0 + mod(scale1)), normed, inv_std)
        d_mid = (cot_ref[at, :].astype(F32) + term).astype(BF16)
        mid[at, :] = d_mid
        g0[at, :] = (mod(gate0) * d_mid.astype(F32)).astype(BF16)

    by_rows(temporal_back)

    flip(g0, gt0)
    shared0.append(send(gt0, sib_gt0, sibling))
    d_att0 = nt(g0[...], wo0[...]).astype(BF16)
    for h in range(HEADS):
        grads = attend_back(part(0, h), part(1, h), part(2, h), probs[h], d_att0[:, h * HD : (h + 1) * HD])
        for n, part_of in enumerate(grads):
            b0[h, :, n * HD : (n + 1) * HD] = part_of
    shared0.append(send(b0.at[1 - core], sib_b0, sibling))
    next(steps1)
    gather_heads(b0)
    arrived(shared0)
    weight_sums(t0, ht0, gt0, b0, sib_ht0, sib_gt0, sib_b0)
    steps0 = reduction(boxes[0], t0)
    next(steps0)
    next(steps1)
    input_back(w0)

    def spatial_back(at):
        normed, inv_std = normalize(x_ref[at, :].astype(F32))
        term = norm_back(acc[at, :] * (1.0 + mod(scale0)), normed, inv_std)
        grad_ref[at, :] = (mid[at, :].astype(F32) + term).astype(BF16)

    next(steps0)
    next(steps1)
    by_rows(spatial_back)
    next(steps0)
    next(steps1)
    next(steps0)
    total1 = next(steps1)
    next(steps0)
    total0 = next(steps0)

    slots, held_rows = 8 * 4 * SLOT, 2 * (X_ROWS // 2) + Z_ROWS
    half = X_ROWS // 2
    hf = lax.rem(z, 2)
    slot = lax.broadcasted_iota(jnp.int32, (slots, held_rows), 0)
    at = lax.broadcasted_iota(jnp.int32, (slots, held_rows), 1)
    edge = X_ROWS * x_hi + half * hf
    turn_of = lax.bitwise_and(lax.shift_right_logical(at, 3), 1)
    last_rows = jnp.where(turn_of == x_hi, at - 2 * half + 4 * X_ROWS + Z_ROWS * hf, -1)
    have = jnp.where(at < half, at + edge, jnp.where(at < 2 * half, at - half + 2 * X_ROWS + edge, last_rows))
    within = lax.bitwise_and(slot, SLOT - 1)
    want = lax.shift_right_logical(slot, 4) * OWN + within
    pick = jnp.where((have == want) & (within < OWN), 1.0, 0.0).astype(BF16)
    for b, total in enumerate((total0, total1)):
        spread[:, b] = nn(pick, total).astype(BF16).reshape(8, 4 * SLOT, HD)
    gathers = [send(spread.at[turn(z, k, 8)], gather.at[z], z_peers[k]) for k in z_order]
    gather[z] = spread[z]
    arrived(gathers)
    for u in range(UNITS):
        both = (gather[2 * u].astype(F32) + gather[2 * u + 1].astype(F32)).astype(BF16)
        for b in range(2):
            for n in range(4):
                merged[n, b, u] = both[b, n * SLOT : (n + 1) * SLOT, :]
    finals = [
        send(merged.at[mate_core * 2 + mate_hi], final.at[n], mates[n])
        for n, (mate_core, mate_hi) in enumerate([(1 - core, x_hi), (core, 1 - x_hi), (1 - core, 1 - x_hi)])
    ]
    arrived(finals)
    sums_ref[core] = merged[core * 2 + x_hi].astype(F32) + final[1].astype(F32)
    sums_ref[1 - core] = final[0].astype(F32) + final[2].astype(F32)
    for copy in used:
        copy.wait_send()


def whole(tokens, ids, cotangent, modulation, w_qkv, w_out):
    _, rows, features = tokens.shape
    inner = HEADS * HD

    def vmem(*shape, dtype=BF16):
        return pltpu.VMEM(shape, dtype)

    full = lambda: vmem(rows, features)
    flipped = lambda: vmem(features, rows)
    ring = [vmem(4, X_ROWS, WIDE) for _ in range(5)]
    second = [vmem(3, X_ROWS, WIDE), vmem(X_ROWS, WIDE)]
    reduction = (
        [vmem(features, WIDE)] + ring + ring + second + second + [
            vmem(8, 8, Z_ROWS, HD), vmem(7, 8, Z_ROWS, HD), vmem(8, Z_ROWS, HD),
            vmem(4, 4, Z_ROWS, HD), vmem(3, Z_ROWS, HD),
            vmem(8, X_ROWS, HD), vmem(7, X_ROWS, HD),
        ]
    )
    scratch = [
        full(), full(), vmem(features, 3 * inner), vmem(features, 3 * inner),
        vmem(inner, features), vmem(inner, features),
        full(), full(), full(), full(), full(), vmem(rows, features, dtype=F32),
        vmem(rows, 3 * inner), vmem(HEADS, rows, rows, dtype=F32), vmem(rows, inner),
    ] + [flipped() for _ in range(8)] + [
        vmem(HEADS, rows, WIDE), vmem(HEADS, FRAMES, rows // FRAMES, WIDE),
        vmem(HEADS, rows, WIDE), vmem(HEADS, rows, WIDE),
        vmem(rows, 3 * inner), vmem(HEADS, rows, WIDE), vmem(rows, WIDE), vmem(rows, WIDE),
    ] + reduction + reduction + [
        vmem(8, 2, 4 * SLOT, HD), vmem(8, 2, 4 * SLOT, HD),
        vmem(4, 2, UNITS, SLOT, HD), vmem(3, 2, UNITS, SLOT, HD),
        pltpu.SemaphoreType.DMA((6,)),
        pltpu.SemaphoreType.DMA((160,)),
        pltpu.SemaphoreType.DMA((160,)),
    ]
    in_vmem = pl.BlockSpec(memory_space=pltpu.VMEM)
    anywhere = pl.BlockSpec(memory_space=pl.ANY)
    return pl.pallas_call(
        whole_kernel,
        out_shape=(
            jax.ShapeDtypeStruct((rows, features), BF16),
            jax.ShapeDtypeStruct((2, 2, UNITS, SLOT, HD), F32),
        ),
        in_specs=[anywhere, in_vmem, anywhere, in_vmem, anywhere, anywhere],
        out_specs=(in_vmem, in_vmem),
        scratch_shapes=scratch,
        compiler_params=pltpu.CompilerParams(
            collective_id=0, has_side_effects=True, vmem_limit_bytes=60 * 2**20
        ),
    )(tokens, ids, cotangent, modulation, w_qkv, w_out)


def local(tokens, window_ids, cotangent, modulation, w_qkv, w_out):
    rows = tokens.shape[1]
    d_tokens, sums = whole(tokens, window_ids, cotangent, modulation, w_qkv, w_out)
    factor = 1.0 / math.sqrt(rows * lax.axis_size("seq") * lax.axis_size("rep"))
    sums = (sums[:, :, :, :OWN] * factor).astype(BF16)
    grad_qkv = sums[:, :, :3].transpose(1, 3, 2, 0, 4).reshape(2, OWN, 3 * HEADS * HD)
    grad_out = sums[:, :, 3].transpose(1, 0, 3, 2).reshape(2, HEADS * HD, OWN)
    return (d_tokens[None], grad_qkv, grad_out)


def solution(mesh):
    in_specs = (P("rep", "seq", None), P("rep", "seq"), P("rep", "seq", None), P(), P(), P())
    out_specs = (
        P("rep", "seq", None),
        P(None, ("seq", "rep"), None),
        P(None, None, ("seq", "rep")),
    )
    return jax.shard_map(local, mesh=mesh, in_specs=in_specs, out_specs=out_specs, check_vma=False)
```

time: 426 us -> 105 us (0.25)
  waiting for transfers between devices: 283 us -> 0 us
  Pallas kernels: 0 us -> 99.8 us
  matrix products: 37.3 us -> 0 us
  local copies, waits for them, and re-layouts: 39.9 us -> 3.7 us
  other arithmetic: 29.6 us -> 0.92 us
  between operations: 14.7 us -> 0.66 us
  blocking collectives: 13.2 us -> 0 us
  starting transfers between devices: 5.98 us -> 0 us
    unnamed x2 -> x0, waiting for transfers between devices: 276 us -> none
    pallas_call x0 -> x1, Pallas kernels: none -> 99.8 us  [whole(): pl.pallas_call(whole_kernel, out_shape=(jax.ShapeDtypeStruct((rows, featu...]
    dot_general x35 -> x0, matrix products: 37.3 us -> none  [the longest x12 13.4 us: times_transposed(): lax.dot_general(left, right, (((1,), (1,)), ((), ())), preferred_element_...]
    concatenate x2 -> x0, other arithmetic: 20.4 us -> none  [the longest x1 19.5 us: local(): jnp.concatenate([contract_rows(hidden_s, d_packed_s), contract_rows(hidde...]
    convert_element_type x2 -> x0, local copies, waits for them, and re-layouts: 19.2 us -> none  [the longest x1 19.2 us: local(): sums = jnp.concatenate([contract_rows(hidden_s, d_packed_s), contract_row...]
    concatenate x2 -> x0, local copies, waits for them, and re-layouts: 14.8 us -> none  [the longest x1 12.7 us: local(): jnp.concatenate([contract_rows(hidden_s, d_packed_s), contract_rows(hidde...]
    all_to_all x1 -> x0, blocking collectives: 13.2 us -> none  [exchange(): lax.all_to_all(values, 'seq', split_axis=0, concat_axis=0, tiled=True, ax...]
    all_to_all x1 -> x0, waiting for transfers between devices: 6.92 us -> none  [exchange(): lax.all_to_all(values, 'seq', split_axis=0, concat_axis=0, tiled=True, ax...]
  transfers between devices with their start and end apart: 2 -> 0, of which waited for: 2 -> 0; matrix products, arithmetic and copies ran while one was open for 1% -> 0% of each run, Pallas kernels for 0% -> 0%
where the time goes in v3:
time: 105 us
  Pallas kernels  99.8 us (95%)
  local copies, waits for them, and re-layouts  3.7 us (4%)
    pallas_call x1, Pallas kernels, whole(): pl.pallas_call(whole_kernel, out_shape=(jax.ShapeDtypeStruct((rows, featu...  99.8 us
    unnamed x1, local copies, waits for them, and re-layouts  2.36 us

profile of v3, /device:TPU:1, one launch (start us, length us, event | category | flops | bytes accessed | tf_op | source)
XLA Modules:
  0.0 105.0 jit_solution(20121902413229757)
XLA Ops:
  0.6 99.8 %shard_map.85 = (bf16[256,2304]{1,0:T(8,128)(2,1)}, f32[2,2,4,16,128]{4,3,2,1,0:T(8,128)}) custom-call(bf16[1,256,2304]{2,1,0:T(8,128)(2,1)} %tokens_hbm.1, s32[1,256]{1,0:T(1,128)} %ids_ref.1, bf16[1,256,2304]{2,1,0:T(8,128)(2,1)} %cot_hbm.1, f32[6,2304]{1,0:T(8,128)} %mod_ref.1, bf16[2,2304,768]{2,1,0:T(8,128)(2,1)} %qkv_hbm.1, bf16[2,256,2304]{2,1,0:T(8,128)(2,1)} %out_hbm.1), custom_call_target="tpu_custom_call" | custom-call | tf_op jit(solution)/shard_map/pallas_call | solution.py:541
  100.4 0.9 multiply_convert_fusion
  101.4 0.7 reshape.12
  102.1 0.6 reshape.13
  102.7 2.4 %copy.12 = bf16[1,256,2304]{2,1,0:T(8,128)(2,1)} copy(bf16[1,256,2304]{2,1,0:T(8,128)(2,1)} %bitcast.11) | data formatting | bytes 2359296
  (4 shorter events, 0.0 us)

commit v4 on v3

--- a/solution.py
+++ b/solution.py
@@ -60,15 +60,14 @@
 
 
 def whole_kernel(tokens_hbm, ids_ref, cot_hbm, mod_ref, qkv_hbm, out_hbm,
-                 grad_ref, sums_ref,
+                 grad_hbm, qkv_ref, att_ref,
                  x_ref, cot_ref, w0, w1, wo0, wo1,
                  hid0, hid1, mid, g1, g0, acc, pk0, probs, att0,
-                 ht0, ht1, gt0, gt1, sib_ht0, sib_ht1, sib_gt0, sib_gt1,
-                 out_s, in_s, out_p, back, dp, b0, sib_b1, sib_b0,
+                 left0, left1, out_s, in_s, out_p, back, b0, sib_b1, sib_b0,
                  *rest):
-    per_block = 22
+    per_block = 20
     boxes = [rest[:per_block], rest[per_block : 2 * per_block]]
-    spread, gather, merged, final, load_sem, send_sem, recv_sem = rest[2 * per_block :]
+    held, gather, merged, final, load_sem, send_sem, recv_sem = rest[2 * per_block :]
 
     seq = lax.axis_index("seq")
     x_hi = lax.axis_index("rep")
@@ -107,6 +106,9 @@
         clip.append((frame_at, device(other if cross else x, y_at, z, core)))
     y_far, y_right, y_left = clip[4][1], clip[5][1], clip[6][1]
 
+    x_ring = ((2, x_far), (1, x_right), (3, x_left))
+    y_ring = ((2, y_far), (1, y_right), (3, y_left))
+
     barrier = pltpu.get_barrier_semaphore()
     peers = [x_right, x_left] + mates + list(z_peers.values()) + [peer for _, peer in clip]
     for peer in peers:
@@ -140,9 +142,9 @@
             body(pl.ds(pl.multiple_of(i * 16, 16), 16))
             return carry
 
-        lax.fori_loop(0, rows_of // 16, step, 0)
-
-    def by_columns(body, size=256):
+        lax.fori_loop(0, rows_of // 16, step, 0, unroll=8)
+
+    def by_columns(body, size=1152):
         def step(i, carry):
             body(pl.ds(pl.multiple_of(i * size, size), size))
             return carry
@@ -176,7 +178,7 @@
         probs[h] = p
         att = nn(p.astype(BF16), part(2, h)).astype(BF16)
         att0[:, h * HD : (h + 1) * HD] = att
-        b0[h, :, 3 * HD :] = att
+        b0[h, 3] = att
     loads[2].wait()
 
     def middle(at):
@@ -200,65 +202,73 @@
     loads[4].wait()
     d_att1 = nt(g1[...], wo1[...]).astype(BF16)
     for h in range(HEADS):
-        out_s[h, :, 3 * HD :] = d_att1[:, h * HD : (h + 1) * HD]
-    loads[5].wait()
-
-    def project1(i, carry):
-        packed = nn(hid1[...], w1[:, pl.ds(pl.multiple_of(i * 256, 256), 256)]).astype(BF16)
-        at = pl.ds(pl.multiple_of(i * HD, HD), HD)
-        for h in range(HEADS):
-            out_s[h, :, at] = packed[:, h * HD : (h + 1) * HD]
-        return carry
-
-    lax.fori_loop(0, 3, project1, 0)
+        out_s[h, 3] = d_att1[:, h * HD : (h + 1) * HD]
 
     pixels = rows_of // FRAMES
 
     def pixel_rows(n):
         return pl.ds(pl.multiple_of(n * pixels, pixels), pixels)
 
+    mine_rows, heads, first_kinds = pixel_rows(frame), pl.ds(0, HEADS), pl.ds(0, 3)
     pl.semaphore_wait(barrier, len(peers))
+    gone_d = [
+        send(out_s.at[heads, 3, pixel_rows(at)], in_s.at[heads, 3, mine_rows], peer) for at, peer in clip
+    ]
+    loads[5].wait()
+    packed = nn(hid1[...], w1[...]).astype(BF16)
+    for n in range(3):
+        for h in range(HEADS):
+            out_s[h, n] = packed[:, (2 * n + h) * HD : (2 * n + h + 1) * HD]
     gone = [
-        [send(out_s.at[h, pixel_rows(at)], in_s.at[h, frame], peer) for at, peer in clip]
+        [
+            send(out_s.at[h, first_kinds, pixel_rows(at)], in_s.at[h, first_kinds, mine_rows], peer)
+            for at, peer in clip
+        ]
         for h in range(HEADS)
     ]
 
-    def flip(src, dst):
-        def body(at):
-            dst[at, :] = src[:, at].T
-
-        by_columns(body)
-
-    flip(hid1, ht1)
-    shared1 = [send(ht1, sib_ht1, sibling)]
-    flip(g1, gt1)
-    shared1.append(send(gt1, sib_gt1, sibling))
+    order = (0, 4, 1, 5, 2, 6, 3, 7, 8, 12, 9, 13, 10, 14, 11, 15, 16, 17)
+    own_tokens, sib_tokens = pl.ds(0, rows_of), pl.ds(rows_of, rows_of)
+
+    def flip(src, dst, n):
+        size = 4 * BLOCK_ROWS
+        for top in range(0, features, size):
+            turned = src[:, top : top + size].T
+            for block in range(0, size, BLOCK_ROWS):
+                for at, tile in enumerate(order):
+                    dst[n, top + block + at * 16 : top + block + at * 16 + 16, 0:rows_of] = turned[
+                        block + tile * 16 : block + tile * 16 + 16, :
+                    ]
+        return send(dst.at[n, :, own_tokens], dst.at[n, :, sib_tokens], sibling)
+
+    shared1 = [flip(hid1, left1, 0), flip(g1, left1, 1)]
 
     pixel_row = lax.bitwise_and(lax.broadcasted_iota(jnp.int32, (rows_of, rows_of), 0), pixels - 1)
     pixel_col = lax.bitwise_and(lax.broadcasted_iota(jnp.int32, (rows_of, rows_of), 1), pixels - 1)
     same_pixel = pixel_row == pixel_col
     came = []
+    arrived(gone_d)
     for h in range(HEADS):
-        in_s[h, frame] = out_s[h, pixel_rows(frame), :]
+        in_s[h, :, mine_rows, :] = out_s[h, :, mine_rows, :]
         arrived(gone[h])
-        block = in_s[h].reshape(rows_of, WIDE)
-        query, key, value, d_out = [block[:, n * HD : (n + 1) * HD] for n in range(UNITS)]
+        query, key, value, d_out = [in_s[h, n] for n in range(UNITS)]
         p = softmax(query, key, same_pixel)
-        out_p[h, :, 3 * HD :] = nn(p.astype(BF16), value).astype(BF16)
+        out_p[h, 3] = nn(p.astype(BF16), value).astype(BF16)
         for n, part_of in enumerate(attend_back(query, key, value, p, d_out)):
-            out_p[h, :, n * HD : (n + 1) * HD] = part_of
+            out_p[h, n] = part_of
         came.append([
-            send(out_p.at[h, pixel_rows(at)], back.at[h, pixel_rows(frame)], peer) for at, peer in clip
+            send(out_p.at[h, :, pixel_rows(at)], back.at[h, :, mine_rows], peer) for at, peer in clip
         ])
-    flip(hid0, ht0)
-    shared0 = [send(ht0, sib_ht0, sibling)]
+    shared0 = [flip(hid0, left0, 0)]
     for h in range(HEADS):
-        back[h, pixel_rows(frame), :] = out_p[h, pixel_rows(frame), :]
+        back[h, :, mine_rows, :] = out_p[h, :, mine_rows, :]
         arrived(came[h])
-    shared1.append(send(back.at[1 - core], sib_b1, sibling))
-
-    def reduction(box, t):
-        (_, xa, xc, xm, xb, xu, ya, yc, ym, yb, yu, x2, x2m, y2, y2m, tz, zr, zu, zx, zy, last_out, last_in) = box
+    kinds = pl.ds(pl.multiple_of(2 * core, 2), 2)
+    sib_kinds = pl.ds(pl.multiple_of(2 * (1 - core), 2), 2)
+    shared1.append(send(back.at[heads, sib_kinds], sib_b1, sibling))
+
+    def reduction(box, t, b):
+        (_, xa, xc, xm, xb, xu, ya, yc, ym, yb, yu, x2, y2, tz, zr, zu, zx, zy, last_out, last_in) = box
 
         def rows(x_at, y_at, offset):
             start = (lax.rem(x_at, 2) * 4 + y_at) * BLOCK_ROWS + offset + X_ROWS * lax.div(x_at, 2)
@@ -302,28 +312,16 @@
                 ).astype(BF16)
 
         half = X_ROWS // 2
-        lo, hi = pl.ds(0, half), pl.ds(half, half)
-
-        def second_start(me, held, into, right, left):
-            far = turn(me, 2, 4)
-            return [
-                send(held.at[far, lo], into.at[0, lo], right),
-                send(held.at[far, hi], into.at[0, hi], left),
-                send(held.at[turn(me, 1, 4), hi], into.at[1, hi], right),
-                send(held.at[turn(me, 3, 4), lo], into.at[1, lo], left),
-            ]
-
-        def second_relay(me, held, into, kept, copies, right, left):
-            copies[0].wait_recv()
-            kept[lo, :] = total2(into[0, lo, :], held[turn(me, 1, 4), lo, :])
-            one = send(kept.at[lo], into.at[2, lo], right)
-            copies[1].wait_recv()
-            kept[hi, :] = total2(into[0, hi, :], held[turn(me, 3, 4), hi, :])
-            return [one, send(kept.at[hi], into.at[2, hi], left)]
-
-        def second_finish(me, held, into, copies, offset):
+
+        def second_start(me, kept, into, ring):
+            return [send(kept.at[turn(me, k, 4)], into.at[n], peer) for n, (k, peer) in enumerate(ring)]
+
+        def second_finish(me, kept, into, copies, offset):
             arrived(copies)
-            total = (held[me].astype(F32) + into[1].astype(F32) + into[2].astype(F32)).astype(BF16)
+            total = kept[me].astype(F32)
+            for n in range(3):
+                total = total + into[n].astype(F32)
+            total = total.astype(BF16)
             for u in range(UNITS):
                 for hf in range(2):
                     last_out[2 * u + hf, offset : offset + half, :] = total[
@@ -346,9 +344,9 @@
             y_relays = relay(y, y_src, ya, ym, yc, y_far_sends, y_right, y_left)
             yield
             finish(x, x_src, xb, xc, x_near + x_relays, xu)
-            x_second = second_start(y, xu, x2, y_right, y_left)
+            x_second = second_start(y, xu, x2, y_ring)
             finish(y, y_src, yb, yc, y_near + y_relays, yu)
-            y_second = second_start(x, yu, y2, x_right, x_left)
+            y_second = second_start(x, yu, y2, x_ring)
             arrived(z_sends)
             total = tz[z].astype(F32)
             for k in range(7):
@@ -364,68 +362,60 @@
                 send(zu.at[quad(1 - x_lo)], zx.at[2], x_left),
             ]
             yield
-            x_more = second_relay(y, xu, x2, x2m, x_second, y_right, y_left)
-            y_more = second_relay(x, yu, y2, y2m, y_second, x_right, x_left)
+            second_finish(y, xu, x2, x_second, 0)
+            second_finish(x, yu, y2, y_second, half)
+            last = [send(last_out.at[turn(z, k, 8)], last_in.at[k - 1], z_peers[k]) for k in z_order]
             arrived(z_first)
             total = zu[quad(x_lo)].astype(F32)
             for n in range(3):
                 total = total + zx[n].astype(F32)
             zx[3] = total.astype(BF16)
-            z_second = [
-                send(zx.at[3, turn(y, 2, 4)], zy.at[0], y_far),
-                send(zx.at[3, turn(y, 1, 4)], zy.at[1], y_right),
-                send(zx.at[3, turn(y, 3, 4)], zy.at[2], y_left),
-            ]
-            yield
-            second_finish(y, xu, x2, x_second[2:] + x_more, 0)
-            second_finish(x, yu, y2, y_second[2:] + y_more, half)
-            last = [send(last_out.at[turn(z, k, 8)], last_in.at[k - 1], z_peers[k]) for k in z_order]
-            arrived(z_second)
-            z_total = zx[3, y].astype(F32)
-            for n in range(3):
-                z_total = z_total + zy[n].astype(F32)
+            z_second = [send(zx.at[3, turn(y, k, 4)], zy.at[n], peer) for n, (k, peer) in enumerate(y_ring)]
             yield
             arrived(last)
             total = last_out[z].astype(F32)
             for k in range(7):
                 total = total + last_in[k].astype(F32)
-            yield jnp.concatenate([total, z_total], axis=0).astype(BF16)
+            for k in range(4):
+                held[k, b] = total[k * SLOT : (k + 1) * SLOT, :].astype(BF16)
+            arrived(z_second)
+            total = zx[3, y].astype(F32)
+            for n in range(3):
+                total = total + zy[n].astype(F32)
+            held[4, b] = total.astype(BF16)
+            yield
 
         return start()
 
-    def weight_sums(t, ht, gt, mine, sib_ht, sib_gt, theirs):
-        head_qkv, head_att = pl.ds(0, 3 * HD), pl.ds(3 * HD, HD)
-
-        def body(i, carry):
-            at = pl.ds(pl.multiple_of(i * BLOCK_ROWS, BLOCK_ROWS), BLOCK_ROWS)
-            t[at, head_qkv] = (
-                nn(ht[at, :], mine[core, :, head_qkv]) + nn(sib_ht[at, :], theirs[:, head_qkv])
-            ).astype(BF16)
-            t[at, head_att] = (
-                nn(gt[at, :], mine[core, :, head_att]) + nn(sib_gt[at, :], theirs[:, head_att])
-            ).astype(BF16)
-            return carry
-
-        lax.fori_loop(0, features // BLOCK_ROWS, body, 0)
-
-    def gather_heads(src):
-        for n in range(3):
-            for h in range(HEADS):
-                dp[:, (2 * n + h) * HD : (2 * n + h + 1) * HD] = src[h, :, n * HD : (n + 1) * HD]
-
-    gather_heads(back)
-
-    def input_back(weight):
+    def weight_sums(t, left, own, theirs):
+        for n in range(2):
+            right = jnp.concatenate(
+                [
+                    jnp.concatenate([own[h, 2 * core + n] for h in range(HEADS)], axis=1),
+                    jnp.concatenate([theirs[h, n] for h in range(HEADS)], axis=1),
+                ],
+                axis=0,
+            )
+            source = core if n == 1 else 0
+
+            def body(at):
+                t[at, 2 * n * HD : 2 * (n + 1) * HD] = nn(left[source, at, :], right).astype(BF16)
+
+            by_columns(body)
+
+    def input_back(src, weight):
+        d_packed = jnp.concatenate([src[h, n] for n in range(3) for h in range(HEADS)], axis=1)
+
         def body(at):
-            acc[:, at] = nt(dp[...], weight[at, :])
+            acc[:, at] = nt(d_packed, weight[at, :])
 
         by_columns(body)
 
-    input_back(w1)
+    input_back(back, w1)
     t1, t0 = boxes[1][0], boxes[0][0]
     arrived(shared1)
-    weight_sums(t1, ht1, gt1, back, sib_ht1, sib_gt1, sib_b1)
-    steps1 = reduction(boxes[1], t1)
+    weight_sums(t1, left1, back, sib_b1)
+    steps1 = reduction(boxes[1], t1, 1)
     next(steps1)
 
     def temporal_back(at):
@@ -437,67 +427,85 @@
 
     by_rows(temporal_back)
 
-    flip(g0, gt0)
-    shared0.append(send(gt0, sib_gt0, sibling))
+    shared0.append(flip(g0, left0, 1))
     d_att0 = nt(g0[...], wo0[...]).astype(BF16)
     for h in range(HEADS):
         grads = attend_back(part(0, h), part(1, h), part(2, h), probs[h], d_att0[:, h * HD : (h + 1) * HD])
         for n, part_of in enumerate(grads):
-            b0[h, :, n * HD : (n + 1) * HD] = part_of
-    shared0.append(send(b0.at[1 - core], sib_b0, sibling))
+            b0[h, n] = part_of
+    shared0.append(send(b0.at[heads, sib_kinds], sib_b0, sibling))
     next(steps1)
-    gather_heads(b0)
+    input_back(b0, w0)
     arrived(shared0)
-    weight_sums(t0, ht0, gt0, b0, sib_ht0, sib_gt0, sib_b0)
-    steps0 = reduction(boxes[0], t0)
+    weight_sums(t0, left0, b0, sib_b0)
+    steps0 = reduction(boxes[0], t0, 0)
     next(steps0)
     next(steps1)
-    input_back(w0)
 
     def spatial_back(at):
         normed, inv_std = normalize(x_ref[at, :].astype(F32))
         term = norm_back(acc[at, :] * (1.0 + mod(scale0)), normed, inv_std)
-        grad_ref[at, :] = (mid[at, :].astype(F32) + term).astype(BF16)
-
-    next(steps0)
-    next(steps1)
+        mid[at, :] = (mid[at, :].astype(F32) + term).astype(BF16)
+
     by_rows(spatial_back)
+    store = pltpu.make_async_copy(mid, grad_hbm, load_sem.at[0])
+    store.start()
     next(steps0)
     next(steps1)
     next(steps0)
-    total1 = next(steps1)
+    next(steps1)
     next(steps0)
-    total0 = next(steps0)
-
-    slots, held_rows = 8 * 4 * SLOT, 2 * (X_ROWS // 2) + Z_ROWS
-    half = X_ROWS // 2
-    hf = lax.rem(z, 2)
-    slot = lax.broadcasted_iota(jnp.int32, (slots, held_rows), 0)
-    at = lax.broadcasted_iota(jnp.int32, (slots, held_rows), 1)
-    edge = X_ROWS * x_hi + half * hf
-    turn_of = lax.bitwise_and(lax.shift_right_logical(at, 3), 1)
-    last_rows = jnp.where(turn_of == x_hi, at - 2 * half + 4 * X_ROWS + Z_ROWS * hf, -1)
-    have = jnp.where(at < half, at + edge, jnp.where(at < 2 * half, at - half + 2 * X_ROWS + edge, last_rows))
+    next(steps0)
+
+    def tile_for(z_at, group):
+        most = 4 - x_hi
+        ahead = lax.max(36 * z_at + 35 - SLOT * group, 0)
+        return lax.min(lax.div(ahead, 4 * SLOT), most)
+
+    group = 2 * x_hi + lax.rem(z, 2)
+    gathers = [
+        send(held.at[tile_for(turn(z, k, 8), group)], gather.at[z], z_peers[k]) for k in z_order
+    ]
+    gather[z] = held[tile_for(z, group)]
+    slot = lax.broadcasted_iota(jnp.int32, (4 * SLOT, 2 * SLOT), 0)
+    at = lax.broadcasted_iota(jnp.int32, (4 * SLOT, 2 * SLOT), 1)
+    tops = [4 * SLOT * tile_for(z, 2 * x_hi + hf) + SLOT * (2 * x_hi + hf) - 36 * z for hf in range(2)]
+    have = jnp.where(at < SLOT, at + tops[0], at - SLOT + tops[1])
     within = lax.bitwise_and(slot, SLOT - 1)
     want = lax.shift_right_logical(slot, 4) * OWN + within
     pick = jnp.where((have == want) & (within < OWN), 1.0, 0.0).astype(BF16)
-    for b, total in enumerate((total0, total1)):
-        spread[:, b] = nn(pick, total).astype(BF16).reshape(8, 4 * SLOT, HD)
-    gathers = [send(spread.at[turn(z, k, 8)], gather.at[z], z_peers[k]) for k in z_order]
-    gather[z] = spread[z]
     arrived(gathers)
-    for u in range(UNITS):
-        both = (gather[2 * u].astype(F32) + gather[2 * u + 1].astype(F32)).astype(BF16)
+    tiles = jnp.concatenate(
+        [
+            jnp.concatenate([gather[2 * u + hf, b] for b in range(2) for u in range(UNITS)], axis=1)
+            for hf in range(2)
+        ],
+        axis=0,
+    )
+    owned = nn(pick, tiles).astype(BF16)
+    for n in range(4):
         for b in range(2):
-            for n in range(4):
-                merged[n, b, u] = both[b, n * SLOT : (n + 1) * SLOT, :]
+            for u in range(UNITS):
+                lanes = (b * UNITS + u) * HD
+                merged[n, b, u] = owned[n * SLOT : (n + 1) * SLOT, lanes : lanes + HD]
     finals = [
         send(merged.at[mate_core * 2 + mate_hi], final.at[n], mates[n])
         for n, (mate_core, mate_hi) in enumerate([(1 - core, x_hi), (core, 1 - x_hi), (1 - core, 1 - x_hi)])
     ]
     arrived(finals)
-    sums_ref[core] = merged[core * 2 + x_hi].astype(F32) + final[1].astype(F32)
-    sums_ref[1 - core] = final[0].astype(F32) + final[2].astype(F32)
+    scale = 1.0 / math.sqrt(rows_of * lax.axis_size("seq") * lax.axis_size("rep"))
+    same = (merged[core * 2 + x_hi].astype(F32) + final[1].astype(F32)) * scale
+    others = (final[0].astype(F32) + final[2].astype(F32)) * scale
+    cores = [jnp.where(core == 0, same, others), jnp.where(core == 0, others, same)]
+    for b in range(2):
+        for c in range(2):
+            for u in range(UNITS):
+                unit = cores[c][b, u]
+                n = c * UNITS + u
+                into, lanes = (qkv_ref, n * HD) if n < 6 else (att_ref, (n - 6) * HD)
+                for i in range(OWN):
+                    into[i, b : b + 1, lanes : lanes + HD] = unit[i : i + 1, :]
+    store.wait()
     for copy in used:
         copy.wait_send()
 
@@ -510,9 +518,10 @@
         return pltpu.VMEM(shape, dtype)
 
     full = lambda: vmem(rows, features)
-    flipped = lambda: vmem(features, rows)
+    pooled = lambda: vmem(2, features, 2 * rows)
+    units = lambda: vmem(HEADS, UNITS, rows, HD)
     ring = [vmem(4, X_ROWS, WIDE) for _ in range(5)]
-    second = [vmem(3, X_ROWS, WIDE), vmem(X_ROWS, WIDE)]
+    second = [vmem(3, X_ROWS, WIDE)]
     reduction = (
         [vmem(features, WIDE)] + ring + ring + second + second + [
             vmem(8, 8, Z_ROWS, HD), vmem(7, 8, Z_ROWS, HD), vmem(8, Z_ROWS, HD),
@@ -525,12 +534,10 @@
         vmem(inner, features), vmem(inner, features),
         full(), full(), full(), full(), full(), vmem(rows, features, dtype=F32),
         vmem(rows, 3 * inner), vmem(HEADS, rows, rows, dtype=F32), vmem(rows, inner),
-    ] + [flipped() for _ in range(8)] + [
-        vmem(HEADS, rows, WIDE), vmem(HEADS, FRAMES, rows // FRAMES, WIDE),
-        vmem(HEADS, rows, WIDE), vmem(HEADS, rows, WIDE),
-        vmem(rows, 3 * inner), vmem(HEADS, rows, WIDE), vmem(rows, WIDE), vmem(rows, WIDE),
+    ] + [pooled(), pooled()] + [units() for _ in range(5)] + [
+        vmem(HEADS, 2, rows, HD), vmem(HEADS, 2, rows, HD),
     ] + reduction + reduction + [
-        vmem(8, 2, 4 * SLOT, HD), vmem(8, 2, 4 * SLOT, HD),
+        vmem(5, 2, SLOT, HD), vmem(8, 2, SLOT, HD),
         vmem(4, 2, UNITS, SLOT, HD), vmem(3, 2, UNITS, SLOT, HD),
         pltpu.SemaphoreType.DMA((6,)),
         pltpu.SemaphoreType.DMA((160,)),
@@ -542,10 +549,11 @@
         whole_kernel,
         out_shape=(
             jax.ShapeDtypeStruct((rows, features), BF16),
-            jax.ShapeDtypeStruct((2, 2, UNITS, SLOT, HD), F32),
+            jax.ShapeDtypeStruct((OWN, 2, 3 * inner), F32),
+            jax.ShapeDtypeStruct((OWN, 2, inner), F32),
         ),
         in_specs=[anywhere, in_vmem, anywhere, in_vmem, anywhere, anywhere],
-        out_specs=(in_vmem, in_vmem),
+        out_specs=(anywhere, in_vmem, in_vmem),
         scratch_shapes=scratch,
         compiler_params=pltpu.CompilerParams(
             collective_id=0, has_side_effects=True, vmem_limit_bytes=60 * 2**20
@@ -553,14 +561,36 @@
     )(tokens, ids, cotangent, modulation, w_qkv, w_out)
 
 
+def hand_over_kernel(grad_hbm, qkv_ref, att_ref, tokens_out, qkv_out, att_out, sems):
+    chunk = grad_hbm.shape[0] // 4
+    copies = []
+    for n in range(4):
+        at = pl.ds(n * chunk, chunk)
+        copies.append(pltpu.make_async_copy(grad_hbm.at[at], tokens_out.at[at], sems.at[n]))
+        copies[n].start()
+    qkv_out[...] = qkv_ref[...].astype(BF16)
+    att_out[...] = att_ref[...].astype(BF16)
+    for copy in copies:
+        copy.wait()
+
+
+def hand_over(grad, qkv, att):
+    in_vmem = pl.BlockSpec(memory_space=pltpu.VMEM)
+    anywhere = pl.BlockSpec(memory_space=pltpu.HBM)
+    return pl.pallas_call(
+        hand_over_kernel,
+        out_shape=tuple(jax.ShapeDtypeStruct(a.shape, BF16) for a in (grad, qkv, att)),
+        in_specs=[anywhere, in_vmem, in_vmem],
+        out_specs=(anywhere, in_vmem, in_vmem),
+        scratch_shapes=[pltpu.SemaphoreType.DMA((4,))],
+    )(grad, qkv, att)
+
+
 def local(tokens, window_ids, cotangent, modulation, w_qkv, w_out):
-    rows = tokens.shape[1]
-    d_tokens, sums = whole(tokens, window_ids, cotangent, modulation, w_qkv, w_out)
-    factor = 1.0 / math.sqrt(rows * lax.axis_size("seq") * lax.axis_size("rep"))
-    sums = (sums[:, :, :, :OWN] * factor).astype(BF16)
-    grad_qkv = sums[:, :, :3].transpose(1, 3, 2, 0, 4).reshape(2, OWN, 3 * HEADS * HD)
-    grad_out = sums[:, :, 3].transpose(1, 0, 3, 2).reshape(2, HEADS * HD, OWN)
-    return (d_tokens[None], grad_qkv, grad_out)
+    d_tokens, qkv, out = hand_over(
+        *whole(tokens, window_ids, cotangent, modulation, w_qkv, w_out)
+    )
+    return (d_tokens[None], qkv.transpose(1, 0, 2), out.transpose(1, 2, 0))
 
 
 def solution(mesh):

time: 105 us -> 121 us (1.15)
  Pallas kernels: 99.8 us -> 120 us
  local copies, waits for them, and re-layouts: 3.7 us -> 0 us
    pallas_call x0 -> x1, Pallas kernels: none -> 38.3 us  [hand_over(): pl.pallas_call(hand_over_kernel, out_shape=tuple((jax.ShapeDtypeStruct(a....]
    pallas_call x1, Pallas kernels: 99.8 us -> 81.9 us  [whole(): pl.pallas_call(whole_kernel, out_shape=(jax.ShapeDtypeStruct((rows, featu...]
    unnamed x1 -> x0, local copies, waits for them, and re-layouts: 2.36 us -> none
    reshape x2 -> x0, local copies, waits for them, and re-layouts: 1.3 us -> none  [the longest x1 0.67 us: local(): sums[:, :, :3].transpose(1, 3, 2, 0, 4).reshape(2, OWN, 3 * HEADS * HD)]
where the time goes in v4:
time: 121 us
  Pallas kernels  120 us (99%)
    pallas_call x1, Pallas kernels, whole(): pl.pallas_call(whole_kernel, out_shape=(jax.ShapeDtypeStruct((rows, featu...  81.9 us
    pallas_call x1, Pallas kernels, hand_over(): pl.pallas_call(hand_over_kernel, out_shape=tuple((jax.ShapeDtypeStruct(a....  38.3 us

profile of v4, /device:TPU:1, one launch (start us, length us, event | category | flops | bytes accessed | tf_op | source)
XLA Modules:
  0.0 121.0 jit_solution(6517006150576629544)
XLA Ops:
  0.6 81.9 %shard_map.85 = (bf16[256,2304]{1,0:T(8,128)(2,1)}, f32[9,2,768]{2,1,0:T(2,128)}, f32[9,2,256]{2,1,0:T(2,128)}) custom-call(bf16[1,256,2304]{2,1,0:T(8,128)(2,1)} %tokens_hbm.1, s32[1,256]{1,0:T(1,128)} %ids_ref.1, bf16[1,256,2304]{2,1,0:T(8,128)(2,1)} %cot_hbm.1, f32[6,2304]{1,0:T(8,128)} %mod_ref.1, bf16[2,2304,768]{2,1,0:T(8,128)(2,1)} %qkv_hbm.1, ...), custom_call_target="tpu_custom_call" | custom-call | tf_op jit(solution)/shard_map/pallas_call | solution.py:548
  82.5 38.3 %shard_map.86 = (bf16[256,2304]{1,0:T(8,128)(2,1)}, bf16[9,2,768]{2,1,0:T(2,128)(2,1)}, bf16[9,2,256]{2,1,0:T(2,128)(2,1)}) custom-call(bf16[256,2304]{1,0:T(8,128)(2,1)} %get-tuple-element.9.grad_hbm, f32[9,2,768]{2,1,0:T(2,128)} %get-tuple-element.10.qkv_ref, f32[9,2,256]{2,1,0:T(2,128)} %get-tuple-element.11.att_ref), custom_call_target="tpu_custom_call" | custom-call | tf_op jit(solution)/shard_map/pallas_call | solution.py:580

commit v5 on v4

--- a/solution.py
+++ b/solution.py
@@ -60,14 +60,14 @@
 
 
 def whole_kernel(tokens_hbm, ids_ref, cot_hbm, mod_ref, qkv_hbm, out_hbm,
-                 grad_hbm, qkv_ref, att_ref,
+                 grad_ref, qkv_ref, att_ref,
                  x_ref, cot_ref, w0, w1, wo0, wo1,
                  hid0, hid1, mid, g1, g0, acc, pk0, probs, att0,
                  left0, left1, out_s, in_s, out_p, back, b0, sib_b1, sib_b0,
                  *rest):
-    per_block = 20
+    per_block = 24
     boxes = [rest[:per_block], rest[per_block : 2 * per_block]]
-    held, gather, merged, final, load_sem, send_sem, recv_sem = rest[2 * per_block :]
+    load_sem, send_sem, recv_sem = rest[2 * per_block :]
 
     seq = lax.axis_index("seq")
     x_hi = lax.axis_index("rep")
@@ -96,8 +96,8 @@
     x_far_at = turn(x, 2, 4)
     z_order = (4, 3, 5, 2, 6, 1, 7)
     z_peers = {k: device(x, y, turn(z, k, 8), core) for k in z_order}
-    mates = [device(x, y, z, 1 - core), device(x_far_at, y, z, core), device(x_far_at, y, z, 1 - core)]
-    sibling, x_far = mates[0], mates[1]
+    sibling, x_far = device(x, y, z, 1 - core), device(x_far_at, y, z, core)
+    far_z_peers = {k: device(x_far_at, y, turn(z, k, 8), core) for k in z_order}
     other = 2 * x_hi + 1 - x_lo
     clip = []
     for cross, step in ((1, 2), (1, 1), (1, 3), (1, 0), (0, 2), (0, 1), (0, 3)):
@@ -110,7 +110,8 @@
     y_ring = ((2, y_far), (1, y_right), (3, y_left))
 
     barrier = pltpu.get_barrier_semaphore()
-    peers = [x_right, x_left] + mates + list(z_peers.values()) + [peer for _, peer in clip]
+    peers = [x_right, x_left, sibling, x_far] + [peer for _, peer in clip]
+    peers += list(z_peers.values()) + list(far_z_peers.values())
     for peer in peers:
         pl.semaphore_signal(barrier, inc=1, device_id=peer, device_id_type=MESH)
 
@@ -160,12 +161,7 @@
     by_rows(spatial_in)
     loads[1].wait()
 
-    def project0(i, carry):
-        at = pl.ds(pl.multiple_of(i * 256, 256), 256)
-        pk0[:, at] = nn(hid0[...], w0[:, at]).astype(BF16)
-        return carry
-
-    lax.fori_loop(0, 3, project0, 0)
+    pk0[...] = nn(hid0[...], w0[...]).astype(BF16)
 
     ids = jnp.broadcast_to(ids_ref[...], (rows_of, rows_of))
     mask = ids == ids.T
@@ -267,8 +263,26 @@
     sib_kinds = pl.ds(pl.multiple_of(2 * (1 - core), 2), 2)
     shared1.append(send(back.at[heads, sib_kinds], sib_b1, sibling))
 
+    def tile_for(z_at, hi_at, half_at):
+        group = 2 * hi_at + half_at
+        ahead = lax.max(36 * z_at + 35 - SLOT * group, 0)
+        return lax.min(lax.div(ahead, 4 * SLOT), 4 - hi_at)
+
+    z_half = lax.rem(z, 2)
+    sources = [(hi_at, half_at) for hi_at in range(2) for half_at in range(2)]
+    slot = lax.broadcasted_iota(jnp.int32, (2 * SLOT, 4 * SLOT), 0)
+    tile_row = lax.broadcasted_iota(jnp.int32, (2 * SLOT, 4 * SLOT), 1)
+    have = lax.bitwise_and(tile_row, SLOT - 1)
+    for n, (hi_at, half_at) in enumerate(sources):
+        top = 4 * SLOT * tile_for(z, hi_at, half_at) + SLOT * (2 * hi_at + half_at) - 36 * z
+        have = jnp.where(lax.shift_right_logical(tile_row, 4) == n, have + top, have)
+    within = lax.bitwise_and(slot, SLOT - 1)
+    want = (2 * lax.shift_right_logical(slot, 4) + x_hi) * OWN + within
+    pick = jnp.where((have == want) & (within < OWN), 1.0, 0.0).astype(BF16)
+
     def reduction(box, t, b):
-        (_, xa, xc, xm, xb, xu, ya, yc, ym, yb, yu, x2, y2, tz, zr, zu, zx, zy, last_out, last_in) = box
+        (_, xa, xc, xm, xb, xu, ya, yc, ym, yb, yu, x2, y2, tz, zr, zu, zx, zy, last_out, last_in,
+         held, gather, merged, final) = box
 
         def rows(x_at, y_at, offset):
             start = (lax.rem(x_at, 2) * 4 + y_at) * BLOCK_ROWS + offset + X_ROWS * lax.div(x_at, 2)
@@ -377,12 +391,41 @@
             for k in range(7):
                 total = total + last_in[k].astype(F32)
             for k in range(4):
-                held[k, b] = total[k * SLOT : (k + 1) * SLOT, :].astype(BF16)
+                held[k] = total[k * SLOT : (k + 1) * SLOT, :].astype(BF16)
             arrived(z_second)
             total = zx[3, y].astype(F32)
             for n in range(3):
                 total = total + zy[n].astype(F32)
-            held[4, b] = total.astype(BF16)
+            held[4] = total.astype(BF16)
+            tiles_out = {k: held.at[tile_for(turn(z, k, 8), x_hi, z_half)] for k in z_order}
+            gathers = [send(tiles_out[k], gather.at[x_hi, z], z_peers[k]) for k in z_order]
+            gathers += [send(tiles_out[k], gather.at[x_hi, z], far_z_peers[k]) for k in z_order]
+            own_tile = held.at[tile_for(z, x_hi, z_half)]
+            gathers.append(send(own_tile, gather.at[x_hi, z], x_far))
+            gather[x_hi, z] = own_tile[...]
+            yield
+            arrived(gathers)
+            tiles = jnp.concatenate(
+                [
+                    jnp.concatenate([gather[hi_at, 2 * u + half_at] for u in range(UNITS)], axis=1)
+                    for hi_at, half_at in sources
+                ],
+                axis=0,
+            )
+            owned = nn(pick, tiles).astype(BF16)
+            for n in range(2):
+                merged[n] = owned[n * SLOT : (n + 1) * SLOT, :]
+            swap = send(merged.at[1 - core], final, sibling)
+            yield
+            scale = 1.0 / math.sqrt(rows_of * lax.axis_size("seq") * lax.axis_size("rep"))
+            same = merged[core].astype(F32) * scale
+            arrived([swap])
+            others = final[...].astype(F32) * scale
+            cores = [jnp.where(core == 0, same, others), jnp.where(core == 0, others, same)]
+            both = jnp.concatenate(cores, axis=1).astype(BF16)
+            for i in range(OWN):
+                qkv_ref[i, b : b + 1, :] = both[i : i + 1, : 6 * HD]
+                att_ref[i, b : b + 1, :] = both[i : i + 1, 6 * HD :]
             yield
 
         return start()
@@ -398,10 +441,7 @@
             )
             source = core if n == 1 else 0
 
-            def body(at):
-                t[at, 2 * n * HD : 2 * (n + 1) * HD] = nn(left[source, at, :], right).astype(BF16)
-
-            by_columns(body)
+            t[:, 2 * n * HD : 2 * (n + 1) * HD] = nn(left[source], right).astype(BF16)
 
     def input_back(src, weight):
         d_packed = jnp.concatenate([src[h, n] for n in range(3) for h in range(HEADS)], axis=1)
@@ -418,11 +458,13 @@
     steps1 = reduction(boxes[1], t1, 1)
     next(steps1)
 
+    d_mid_ref = hid1
+
     def temporal_back(at):
         normed, inv_std = normalize(mid[at, :].astype(F32))
         term = norm_back(acc[at, :] * (1.0 + mod(scale1)), normed, inv_std)
         d_mid = (cot_ref[at, :].astype(F32) + term).astype(BF16)
-        mid[at, :] = d_mid
+        d_mid_ref[at, :] = d_mid
         g0[at, :] = (mod(gate0) * d_mid.astype(F32)).astype(BF16)
 
     by_rows(temporal_back)
@@ -434,78 +476,30 @@
         for n, part_of in enumerate(grads):
             b0[h, n] = part_of
     shared0.append(send(b0.at[heads, sib_kinds], sib_b0, sibling))
-    next(steps1)
     input_back(b0, w0)
+    next(steps1)
     arrived(shared0)
     weight_sums(t0, left0, b0, sib_b0)
     steps0 = reduction(boxes[0], t0, 0)
     next(steps0)
-    next(steps1)
 
     def spatial_back(at):
         normed, inv_std = normalize(x_ref[at, :].astype(F32))
         term = norm_back(acc[at, :] * (1.0 + mod(scale0)), normed, inv_std)
-        mid[at, :] = (mid[at, :].astype(F32) + term).astype(BF16)
+        grad_ref[at, :] = (d_mid_ref[at, :].astype(F32) + term).astype(BF16)
 
     by_rows(spatial_back)
-    store = pltpu.make_async_copy(mid, grad_hbm, load_sem.at[0])
-    store.start()
-    next(steps0)
-    next(steps1)
-    next(steps0)
-    next(steps1)
-    next(steps0)
-    next(steps0)
-
-    def tile_for(z_at, group):
-        most = 4 - x_hi
-        ahead = lax.max(36 * z_at + 35 - SLOT * group, 0)
-        return lax.min(lax.div(ahead, 4 * SLOT), most)
-
-    group = 2 * x_hi + lax.rem(z, 2)
-    gathers = [
-        send(held.at[tile_for(turn(z, k, 8), group)], gather.at[z], z_peers[k]) for k in z_order
-    ]
-    gather[z] = held[tile_for(z, group)]
-    slot = lax.broadcasted_iota(jnp.int32, (4 * SLOT, 2 * SLOT), 0)
-    at = lax.broadcasted_iota(jnp.int32, (4 * SLOT, 2 * SLOT), 1)
-    tops = [4 * SLOT * tile_for(z, 2 * x_hi + hf) + SLOT * (2 * x_hi + hf) - 36 * z for hf in range(2)]
-    have = jnp.where(at < SLOT, at + tops[0], at - SLOT + tops[1])
-    within = lax.bitwise_and(slot, SLOT - 1)
-    want = lax.shift_right_logical(slot, 4) * OWN + within
-    pick = jnp.where((have == want) & (within < OWN), 1.0, 0.0).astype(BF16)
-    arrived(gathers)
-    tiles = jnp.concatenate(
-        [
-            jnp.concatenate([gather[2 * u + hf, b] for b in range(2) for u in range(UNITS)], axis=1)
-            for hf in range(2)
-        ],
-        axis=0,
-    )
-    owned = nn(pick, tiles).astype(BF16)
-    for n in range(4):
-        for b in range(2):
-            for u in range(UNITS):
-                lanes = (b * UNITS + u) * HD
-                merged[n, b, u] = owned[n * SLOT : (n + 1) * SLOT, lanes : lanes + HD]
-    finals = [
-        send(merged.at[mate_core * 2 + mate_hi], final.at[n], mates[n])
-        for n, (mate_core, mate_hi) in enumerate([(1 - core, x_hi), (core, 1 - x_hi), (1 - core, 1 - x_hi)])
-    ]
-    arrived(finals)
-    scale = 1.0 / math.sqrt(rows_of * lax.axis_size("seq") * lax.axis_size("rep"))
-    same = (merged[core * 2 + x_hi].astype(F32) + final[1].astype(F32)) * scale
-    others = (final[0].astype(F32) + final[2].astype(F32)) * scale
-    cores = [jnp.where(core == 0, same, others), jnp.where(core == 0, others, same)]
-    for b in range(2):
-        for c in range(2):
-            for u in range(UNITS):
-                unit = cores[c][b, u]
-                n = c * UNITS + u
-                into, lanes = (qkv_ref, n * HD) if n < 6 else (att_ref, (n - 6) * HD)
-                for i in range(OWN):
-                    into[i, b : b + 1, lanes : lanes + HD] = unit[i : i + 1, :]
-    store.wait()
+    next(steps0)
+    next(steps1)
+    next(steps0)
+    next(steps1)
+    next(steps0)
+    next(steps1)
+    next(steps0)
+    next(steps1)
+    next(steps0)
+    next(steps1)
+    next(steps0)
     for copy in used:
         copy.wait_send()
 
@@ -527,6 +521,7 @@
             vmem(8, 8, Z_ROWS, HD), vmem(7, 8, Z_ROWS, HD), vmem(8, Z_ROWS, HD),
             vmem(4, 4, Z_ROWS, HD), vmem(3, Z_ROWS, HD),
             vmem(8, X_ROWS, HD), vmem(7, X_ROWS, HD),
+            vmem(5, SLOT, HD), vmem(2, 8, SLOT, HD), vmem(2, SLOT, WIDE), vmem(SLOT, WIDE),
         ]
     )
     scratch = [
@@ -537,23 +532,21 @@
     ] + [pooled(), pooled()] + [units() for _ in range(5)] + [
         vmem(HEADS, 2, rows, HD), vmem(HEADS, 2, rows, HD),
     ] + reduction + reduction + [
-        vmem(5, 2, SLOT, HD), vmem(8, 2, SLOT, HD),
-        vmem(4, 2, UNITS, SLOT, HD), vmem(3, 2, UNITS, SLOT, HD),
         pltpu.SemaphoreType.DMA((6,)),
-        pltpu.SemaphoreType.DMA((160,)),
-        pltpu.SemaphoreType.DMA((160,)),
+        pltpu.SemaphoreType.DMA((176,)),
+        pltpu.SemaphoreType.DMA((176,)),
     ]
     in_vmem = pl.BlockSpec(memory_space=pltpu.VMEM)
     anywhere = pl.BlockSpec(memory_space=pl.ANY)
     return pl.pallas_call(
         whole_kernel,
         out_shape=(
-            jax.ShapeDtypeStruct((rows, features), BF16),
-            jax.ShapeDtypeStruct((OWN, 2, 3 * inner), F32),
-            jax.ShapeDtypeStruct((OWN, 2, inner), F32),
+            pltpu.VMEM((rows, features), BF16),
+            pltpu.VMEM((OWN, 2, 3 * inner), BF16),
+            pltpu.VMEM((OWN, 2, inner), BF16),
         ),
         in_specs=[anywhere, in_vmem, anywhere, in_vmem, anywhere, anywhere],
-        out_specs=(anywhere, in_vmem, in_vmem),
+        out_specs=(in_vmem, in_vmem, in_vmem),
         scratch_shapes=scratch,
         compiler_params=pltpu.CompilerParams(
             collective_id=0, has_side_effects=True, vmem_limit_bytes=60 * 2**20
@@ -561,35 +554,8 @@
     )(tokens, ids, cotangent, modulation, w_qkv, w_out)
 
 
-def hand_over_kernel(grad_hbm, qkv_ref, att_ref, tokens_out, qkv_out, att_out, sems):
-    chunk = grad_hbm.shape[0] // 4
-    copies = []
-    for n in range(4):
-        at = pl.ds(n * chunk, chunk)
-        copies.append(pltpu.make_async_copy(grad_hbm.at[at], tokens_out.at[at], sems.at[n]))
-        copies[n].start()
-    qkv_out[...] = qkv_ref[...].astype(BF16)
-    att_out[...] = att_ref[...].astype(BF16)
-    for copy in copies:
-        copy.wait()
-
-
-def hand_over(grad, qkv, att):
-    in_vmem = pl.BlockSpec(memory_space=pltpu.VMEM)
-    anywhere = pl.BlockSpec(memory_space=pltpu.HBM)
-    return pl.pallas_call(
-        hand_over_kernel,
-        out_shape=tuple(jax.ShapeDtypeStruct(a.shape, BF16) for a in (grad, qkv, att)),
-        in_specs=[anywhere, in_vmem, in_vmem],
-        out_specs=(anywhere, in_vmem, in_vmem),
-        scratch_shapes=[pltpu.SemaphoreType.DMA((4,))],
-    )(grad, qkv, att)
-
-
 def local(tokens, window_ids, cotangent, modulation, w_qkv, w_out):
-    d_tokens, qkv, out = hand_over(
-        *whole(tokens, window_ids, cotangent, modulation, w_qkv, w_out)
-    )
+    d_tokens, qkv, out = whole(tokens, window_ids, cotangent, modulation, w_qkv, w_out)
     return (d_tokens[None], qkv.transpose(1, 0, 2), out.transpose(1, 2, 0))
 
 

time: 121 us -> 80.2 us (0.66)
  Pallas kernels: 120 us -> 77.3 us
  local copies, waits for them, and re-layouts: 0 us -> 2.22 us
    pallas_call x2 -> x1, Pallas kernels: 120 us -> 77.3 us  [whole(): pl.pallas_call(whole_kernel, out_shape=(pltpu.VMEM((rows, features), BF16...]
    unnamed x0 -> x3, local copies, waits for them, and re-layouts: none -> 2.22 us
where the time goes in v5:
time: 80.2 us; the launch traced here: 80.1 us
  Pallas kernels  77.3 us (96%)
  local copies, waits for them, and re-layouts  2.22 us (3%)
    pallas_call x1, Pallas kernels, whole(): pl.pallas_call(whole_kernel, out_shape=(pltpu.VMEM((rows, features), BF16...  77.3 us
    unnamed x3, local copies, waits for them, and re-layouts  2.22 us

profile of v5, /device:TPU:1, one launch (start us, length us, event | category | flops | bytes accessed | tf_op | source)
XLA Modules:
  0.0 80.1 jit_solution(7609074669352231505)
XLA Ops:
  0.6 77.3 %shard_map.85 = (bf16[256,2304]{1,0:T(8,128)(2,1)S(1)}, bf16[9,2,768]{2,1,0:T(2,128)(2,1)S(1)}, bf16[9,2,256]{2,1,0:T(2,128)(2,1)S(1)}) custom-call(bf16[1,256,2304]{2,1,0:T(8,128)(2,1)} %tokens_hbm.1, s32[1,256]{1,0:T(1,128)} %ids_ref.1, bf16[1,256,2304]{2,1,0:T(8,128)(2,1)} %cot_hbm.1, f32[6,2304]{1,0:T(8,128)} %mod_ref.1, bf16[2,2304,768]{2,1,0:T(8,128)(2,1)} %qkv_hbm.1, ...), custom_call_target="tpu_custom_call" | custom-call | tf_op jit(solution)/shard_map/pallas_call | solution.py:541
  77.9 1.0 %copy.12 = bf16[1,256,2304]{2,1,0:T(8,128)(2,1)} copy(bf16[1,256,2304]{2,1,0:T(8,128)(2,1)S(1)} %bitcast.3) | data formatting | bytes 2359296
  78.9 0.6 copy.13
  79.5 0.6 copy.14

commit v6 on v5

--- a/solution.py
+++ b/solution.py
@@ -78,13 +78,28 @@
     x = 2 * x_hi + x_lo
     frame = x_lo * 4 + y
 
-    loads = []
-    for n, (src, dst) in enumerate([
-        (tokens_hbm.at[0], x_ref), (qkv_hbm.at[0], w0), (out_hbm.at[0], wo0),
-        (cot_hbm.at[0], cot_ref), (out_hbm.at[1], wo1), (qkv_hbm.at[1], w1),
-    ]):
-        loads.append(pltpu.make_async_copy(src, dst, load_sem.at[n]))
-        loads[n].start()
+    loads, load_count = [], 0
+    for src, dst, pieces in [
+        (tokens_hbm.at[0], x_ref, 1), (qkv_hbm.at[0], w0, 4), (out_hbm.at[0], wo0, 1),
+        (cot_hbm.at[0], cot_ref, 1), (out_hbm.at[1], wo1, 1), (qkv_hbm.at[1], w1, 4),
+    ]:
+        size = dst.shape[0] // pieces
+        loads.append([])
+        for n in range(pieces):
+            at = pl.ds(n * size, size)
+            loads[-1].append(pltpu.make_async_copy(src.at[at], dst.at[at], load_sem.at[load_count]))
+            load_count += 1
+
+    def begin(*which):
+        for n in which:
+            for copy in loads[n]:
+                copy.start()
+
+    def loaded(n):
+        for copy in loads[n]:
+            copy.wait()
+
+    begin(0, 1)
 
     def device(x_at, y_at, z_at, core_at):
         return {"seq": ((lax.rem(x_at, 2) * 4 + y_at) * 8 + z_at) * 2 + core_at, "rep": lax.div(x_at, 2)}
@@ -131,6 +146,13 @@
         for copy in copies:
             copy.wait_recv()
 
+    gone_already = []
+
+    def departed(copies):
+        for copy in copies:
+            copy.wait_send()
+        gone_already.extend(copies)
+
     rows_of = x_ref.shape[0]
     features = x_ref.shape[1]
     shift0, scale0, gate0, shift1, scale1, gate1 = range(6)
@@ -152,14 +174,15 @@
 
         lax.fori_loop(0, features // size, step, 0)
 
-    loads[0].wait()
+    loaded(0)
 
     def spatial_in(at):
         normed, _ = normalize(x_ref[at, :].astype(F32))
         hid0[at, :] = (normed * (1.0 + mod(scale0)) + mod(shift0)).astype(BF16)
 
     by_rows(spatial_in)
-    loads[1].wait()
+    loaded(1)
+    begin(2, 3, 4, 5)
 
     pk0[...] = nn(hid0[...], w0[...]).astype(BF16)
 
@@ -175,7 +198,7 @@
         att = nn(p.astype(BF16), part(2, h)).astype(BF16)
         att0[:, h * HD : (h + 1) * HD] = att
         b0[h, 3] = att
-    loads[2].wait()
+    loaded(2)
 
     def middle(at):
         mid[:, at] = (
@@ -189,13 +212,13 @@
         hid1[at, :] = (normed * (1.0 + mod(scale1)) + mod(shift1)).astype(BF16)
 
     by_rows(temporal_in)
-    loads[3].wait()
+    loaded(3)
 
     def gate_top(at):
         g1[at, :] = (mod(gate1) * cot_ref[at, :].astype(F32)).astype(BF16)
 
     by_rows(gate_top)
-    loads[4].wait()
+    loaded(4)
     d_att1 = nt(g1[...], wo1[...]).astype(BF16)
     for h in range(HEADS):
         out_s[h, 3] = d_att1[:, h * HD : (h + 1) * HD]
@@ -210,18 +233,19 @@
     gone_d = [
         send(out_s.at[heads, 3, pixel_rows(at)], in_s.at[heads, 3, mine_rows], peer) for at, peer in clip
     ]
-    loads[5].wait()
+    loaded(5)
     packed = nn(hid1[...], w1[...]).astype(BF16)
     for n in range(3):
         for h in range(HEADS):
             out_s[h, n] = packed[:, (2 * n + h) * HD : (2 * n + h + 1) * HD]
-    gone = [
-        [
+
+    def send_head(h):
+        return [
             send(out_s.at[h, first_kinds, pixel_rows(at)], in_s.at[h, first_kinds, mine_rows], peer)
             for at, peer in clip
         ]
-        for h in range(HEADS)
-    ]
+
+    gone = [send_head(0)]
 
     order = (0, 4, 1, 5, 2, 6, 3, 7, 8, 12, 9, 13, 10, 14, 11, 15, 16, 17)
     own_tokens, sib_tokens = pl.ds(0, rows_of), pl.ds(rows_of, rows_of)
@@ -238,6 +262,8 @@
         return send(dst.at[n, :, own_tokens], dst.at[n, :, sib_tokens], sibling)
 
     shared1 = [flip(hid1, left1, 0), flip(g1, left1, 1)]
+    departed(gone[0])
+    gone.append(send_head(1))
 
     pixel_row = lax.bitwise_and(lax.broadcasted_iota(jnp.int32, (rows_of, rows_of), 0), pixels - 1)
     pixel_col = lax.bitwise_and(lax.broadcasted_iota(jnp.int32, (rows_of, rows_of), 1), pixels - 1)
@@ -345,14 +371,15 @@
         def start():
             x_far_sends = far_sends(x, x_src, xa, x_right, x_left)
             y_far_sends = far_sends(y, y_src, ya, y_right, y_left)
-            x_near = near_sends(x, x_src, xb, x_right, x_left)
-            y_near = near_sends(y, y_src, yb, y_right, y_left)
             for u in range(UNITS):
                 for hf in range(2):
                     for a in range(8):
                         top = a * BLOCK_ROWS + 4 * X_ROWS + Z_ROWS * hf
                         tz[2 * u + hf, a] = t[top : top + Z_ROWS, u * HD : (u + 1) * HD]
             z_sends = [send(tz.at[turn(z, k, 8)], zr.at[k - 1], z_peers[k]) for k in z_order]
+            yield
+            x_near = near_sends(x, x_src, xb, x_right, x_left)
+            y_near = near_sends(y, y_src, yb, y_right, y_left)
             yield
             x_relays = relay(x, x_src, xa, xm, xc, x_far_sends, x_right, x_left)
             y_relays = relay(y, y_src, ya, ym, yc, y_far_sends, y_right, y_left)
@@ -451,12 +478,12 @@
 
         by_columns(body)
 
-    input_back(back, w1)
     t1, t0 = boxes[1][0], boxes[0][0]
     arrived(shared1)
     weight_sums(t1, left1, back, sib_b1)
     steps1 = reduction(boxes[1], t1, 1)
     next(steps1)
+    input_back(back, w1)
 
     d_mid_ref = hid1
 
@@ -468,6 +495,7 @@
         g0[at, :] = (mod(gate0) * d_mid.astype(F32)).astype(BF16)
 
     by_rows(temporal_back)
+    next(steps1)
 
     shared0.append(flip(g0, left0, 1))
     d_att0 = nt(g0[...], wo0[...]).astype(BF16)
@@ -476,7 +504,6 @@
         for n, part_of in enumerate(grads):
             b0[h, n] = part_of
     shared0.append(send(b0.at[heads, sib_kinds], sib_b0, sibling))
-    input_back(b0, w0)
     next(steps1)
     arrived(shared0)
     weight_sums(t0, left0, b0, sib_b0)
@@ -488,6 +515,8 @@
         term = norm_back(acc[at, :] * (1.0 + mod(scale0)), normed, inv_std)
         grad_ref[at, :] = (d_mid_ref[at, :].astype(F32) + term).astype(BF16)
 
+    input_back(b0, w0)
+    next(steps0)
     by_rows(spatial_back)
     next(steps0)
     next(steps1)
@@ -501,7 +530,8 @@
     next(steps1)
     next(steps0)
     for copy in used:
-        copy.wait_send()
+        if not any(copy is other for other in gone_already):
+            copy.wait_send()
 
 
 def whole(tokens, ids, cotangent, modulation, w_qkv, w_out):
@@ -532,7 +562,7 @@
     ] + [pooled(), pooled()] + [units() for _ in range(5)] + [
         vmem(HEADS, 2, rows, HD), vmem(HEADS, 2, rows, HD),
     ] + reduction + reduction + [
-        pltpu.SemaphoreType.DMA((6,)),
+        pltpu.SemaphoreType.DMA((16,)),
         pltpu.SemaphoreType.DMA((176,)),
         pltpu.SemaphoreType.DMA((176,)),
     ]

time: 80.2 us -> 79 us (0.985)
  Pallas kernels: 77.3 us -> 76 us
    pallas_call x1, Pallas kernels: 77.3 us -> 76 us  [whole(): pl.pallas_call(whole_kernel, out_shape=(pltpu.VMEM((rows, features), BF16...]
where the time goes in v6:
time: 79 us; the launch traced here: 78.9 us
  Pallas kernels  76 us (96%)
  local copies, waits for them, and re-layouts  2.22 us (3%)
    pallas_call x1, Pallas kernels, whole(): pl.pallas_call(whole_kernel, out_shape=(pltpu.VMEM((rows, features), BF16...  76 us
    unnamed x3, local copies, waits for them, and re-layouts  2.22 us

profile of v6, /device:TPU:1, one launch (start us, length us, event | category | flops | bytes accessed | tf_op | source)
XLA Modules:
  0.0 78.9 jit_solution(12074581753562023089)
XLA Ops:
  0.6 76.0 %shard_map.85 = (bf16[256,2304]{1,0:T(8,128)(2,1)S(1)}, bf16[9,2,768]{2,1,0:T(2,128)(2,1)S(1)}, bf16[9,2,256]{2,1,0:T(2,128)(2,1)S(1)}) custom-call(bf16[1,256,2304]{2,1,0:T(8,128)(2,1)} %tokens_hbm.1, s32[1,256]{1,0:T(1,128)} %ids_ref.1, bf16[1,256,2304]{2,1,0:T(8,128)(2,1)} %cot_hbm.1, f32[6,2304]{1,0:T(8,128)} %mod_ref.1, bf16[2,2304,768]{2,1,0:T(8,128)(2,1)} %qkv_hbm.1, ...), custom_call_target="tpu_custom_call" | custom-call | tf_op jit(solution)/shard_map/pallas_call | solution.py:571
  76.7 1.0 %copy.12 = bf16[1,256,2304]{2,1,0:T(8,128)(2,1)} copy(bf16[1,256,2304]{2,1,0:T(8,128)(2,1)S(1)} %bitcast.3) | data formatting | bytes 2359296
  77.7 0.6 copy.13
  78.3 0.6 copy.14

commit v7 on v6

--- a/solution.py
+++ b/solution.py
@@ -59,11 +59,11 @@
     )
 
 
-def whole_kernel(tokens_hbm, ids_ref, cot_hbm, mod_ref, qkv_hbm, out_hbm,
+def whole_kernel(tokens_hbm, ids_hbm, cot_hbm, mod_hbm, qkv_hbm, out_hbm,
                  grad_ref, qkv_ref, att_ref,
                  x_ref, cot_ref, w0, w1, wo0, wo1,
                  hid0, hid1, mid, g1, g0, acc, pk0, probs, att0,
-                 left0, left1, out_s, in_s, out_p, back, b0, sib_b1, sib_b0,
+                 ids_ref, mod_ref, left0, left1, out_s, in_s, out_p, back, b0, sib_b1, sib_b0,
                  *rest):
     per_block = 24
     boxes = [rest[:per_block], rest[per_block : 2 * per_block]]
@@ -80,8 +80,9 @@
 
     loads, load_count = [], 0
     for src, dst, pieces in [
-        (tokens_hbm.at[0], x_ref, 1), (qkv_hbm.at[0], w0, 4), (out_hbm.at[0], wo0, 1),
+        (tokens_hbm.at[0], x_ref, 4), (qkv_hbm.at[0], w0, 4), (out_hbm.at[0], wo0, 1),
         (cot_hbm.at[0], cot_ref, 1), (out_hbm.at[1], wo1, 1), (qkv_hbm.at[1], w1, 4),
+        (mod_hbm, mod_ref, 1), (ids_hbm, ids_ref, 1),
     ]:
         size = dst.shape[0] // pieces
         loads.append([])
@@ -99,7 +100,7 @@
         for copy in loads[n]:
             copy.wait()
 
-    begin(0, 1)
+    begin(0, 6, 1, 7)
 
     def device(x_at, y_at, z_at, core_at):
         return {"seq": ((lax.rem(x_at, 2) * 4 + y_at) * 8 + z_at) * 2 + core_at, "rep": lax.div(x_at, 2)}
@@ -174,6 +175,7 @@
 
         lax.fori_loop(0, features // size, step, 0)
 
+    loaded(6)
     loaded(0)
 
     def spatial_in(at):
@@ -186,6 +188,7 @@
 
     pk0[...] = nn(hid0[...], w0[...]).astype(BF16)
 
+    loaded(7)
     ids = jnp.broadcast_to(ids_ref[...], (rows_of, rows_of))
     mask = ids == ids.T
 
@@ -559,10 +562,10 @@
         vmem(inner, features), vmem(inner, features),
         full(), full(), full(), full(), full(), vmem(rows, features, dtype=F32),
         vmem(rows, 3 * inner), vmem(HEADS, rows, rows, dtype=F32), vmem(rows, inner),
-    ] + [pooled(), pooled()] + [units() for _ in range(5)] + [
+    ] + [vmem(1, rows, dtype=jnp.int32), vmem(6, features, dtype=F32), pooled(), pooled()] + [units() for _ in range(5)] + [
         vmem(HEADS, 2, rows, HD), vmem(HEADS, 2, rows, HD),
     ] + reduction + reduction + [
-        pltpu.SemaphoreType.DMA((16,)),
+        pltpu.SemaphoreType.DMA((20,)),
         pltpu.SemaphoreType.DMA((176,)),
         pltpu.SemaphoreType.DMA((176,)),
     ]
@@ -575,7 +578,7 @@
             pltpu.VMEM((OWN, 2, 3 * inner), BF16),
             pltpu.VMEM((OWN, 2, inner), BF16),
         ),
-        in_specs=[anywhere, in_vmem, anywhere, in_vmem, anywhere, anywhere],
+        in_specs=[anywhere] * 6,
         out_specs=(in_vmem, in_vmem, in_vmem),
         scratch_shapes=scratch,
         compiler_params=pltpu.CompilerParams(

time: 79 us -> 78.6 us (level)
  no operation moved by 1% of the time
where the time goes in v7:
time: 78.6 us; the launch traced here: 78.5 us
  Pallas kernels  75.7 us (96%)
  local copies, waits for them, and re-layouts  2.22 us (3%)
    pallas_call x1, Pallas kernels, whole(): pl.pallas_call(whole_kernel, out_shape=(pltpu.VMEM((rows, features), BF16...  75.7 us
    unnamed x3, local copies, waits for them, and re-layouts  2.22 us

profile of v7, /device:TPU:1, one launch (start us, length us, event | category | flops | bytes accessed | tf_op | source)
XLA Modules:
  0.0 78.5 jit_solution(18368067955156754906)
XLA Ops:
  0.6 75.7 %shard_map.85 = (bf16[256,2304]{1,0:T(8,128)(2,1)S(1)}, bf16[9,2,768]{2,1,0:T(2,128)(2,1)S(1)}, bf16[9,2,256]{2,1,0:T(2,128)(2,1)S(1)}) custom-call(bf16[1,256,2304]{2,1,0:T(8,128)(2,1)} %tokens_hbm.1, s32[1,256]{1,0:T(1,128)} %ids_hbm.1, bf16[1,256,2304]{2,1,0:T(8,128)(2,1)} %cot_hbm.1, f32[6,2304]{1,0:T(8,128)} %mod_hbm.1, bf16[2,2304,768]{2,1,0:T(8,128)(2,1)} %qkv_hbm.1, ...), custom_call_target="tpu_custom_call" | custom-call | tf_op jit(solution)/shard_map/pallas_call | solution.py:574
  76.3 1.0 %copy.12 = bf16[1,256,2304]{2,1,0:T(8,128)(2,1)} copy(bf16[1,256,2304]{2,1,0:T(8,128)(2,1)S(1)} %bitcast.3) | data formatting | bytes 2359296
  77.3 0.6 copy.13
  77.9 0.6 copy.14

commit v8 on v7

--- a/solution.py
+++ b/solution.py
@@ -166,9 +166,9 @@
             body(pl.ds(pl.multiple_of(i * 16, 16), 16))
             return carry
 
-        lax.fori_loop(0, rows_of // 16, step, 0, unroll=8)
-
-    def by_columns(body, size=1152):
+        lax.fori_loop(0, rows_of // 16, step, 0, unroll=16)
+
+    def by_columns(body, size=2304):
         def step(i, carry):
             body(pl.ds(pl.multiple_of(i * size, size), size))
             return carry

time: 78.6 us -> 78.2 us (level)
  no operation moved by 1% of the time
where the time goes in v8:
time: 78.2 us
  Pallas kernels  75.3 us (96%)
  local copies, waits for them, and re-layouts  2.22 us (3%)
    pallas_call x1, Pallas kernels, whole(): pl.pallas_call(whole_kernel, out_shape=(pltpu.VMEM((rows, features), BF16...  75.3 us
    unnamed x3, local copies, waits for them, and re-layouts  2.22 us

profile of v8, /device:TPU:1, one launch (start us, length us, event | category | flops | bytes accessed | tf_op | source)
XLA Modules:
  0.0 78.2 jit_solution(13935259305532684562)
XLA Ops:
  0.6 75.3 %shard_map.85 = (bf16[256,2304]{1,0:T(8,128)(2,1)S(1)}, bf16[9,2,768]{2,1,0:T(2,128)(2,1)S(1)}, bf16[9,2,256]{2,1,0:T(2,128)(2,1)S(1)}) custom-call(bf16[1,256,2304]{2,1,0:T(8,128)(2,1)} %tokens_hbm.1, s32[1,256]{1,0:T(1,128)} %ids_hbm.1, bf16[1,256,2304]{2,1,0:T(8,128)(2,1)} %cot_hbm.1, f32[6,2304]{1,0:T(8,128)} %mod_hbm.1, bf16[2,2304,768]{2,1,0:T(8,128)(2,1)} %qkv_hbm.1, ...), custom_call_target="tpu_custom_call" | custom-call | tf_op jit(solution)/shard_map/pallas_call | solution.py:574
  75.9 1.0 %copy.12 = bf16[1,256,2304]{2,1,0:T(8,128)(2,1)} copy(bf16[1,256,2304]{2,1,0:T(8,128)(2,1)S(1)} %bitcast.3) | data formatting | bytes 2359296
  77.0 0.6 copy.13
  77.6 0.6 copy.14
